TPU v7x, 128 devices: a whole 4x4x4 slice. The times are simulated.
128 devices in a mesh: row: 8 (over x, y_lo), col: 8 (over y_hi, z), grp: 2 (over core).
Axes of the slice: x: 4, y: 4 (y_hi: 2, y_lo: 2; y = y_hi * 2 + y_lo), z: 4, core: 2. Of those that a mesh axis runs over, the one named last changes fastest.
Arguments:
- skip: bfloat16 [128, 64, 32, 320], P('grp', 'row', 'col'), may hold values from -6 to 6
- w_up: bfloat16 [9, 320, 320], replicated, may hold values from -0.109375 to 0.109375
- w_in: bfloat16 [320, 1280], replicated, may hold values from -1.25 to 1.25
- w_out: bfloat16 [1280, 320], replicated, may hold values from -0.15625 to 0.15625
- spatial_w: bfloat16 [4, 1280, 640], replicated, may hold values from -0.5310661 to 0.5310661
- temporal_w: bfloat16 [4, 1280, 640], replicated, may hold values from -0.5310661 to 0.5310661
- grad_out: bfloat16 [128, 64, 32, 320], P('grp', 'row', 'col'), may hold values from -32 to 32
Outputs:
- grad_skip: bfloat16 [128, 64, 32, 320], P('grp', 'row', 'col')
- grad_w_up: float32 [9, 320, 320], replicated
- grad_w_in: float32 [320, 1280], replicated
- grad_w_out: float32 [1280, 320], replicated
All inputs are finite; a program needn't handle non-finite values.
Results may differ from a plain program's by a relative error of at most 0.035.
Values may be sent and summed in bfloat16 or wider, within the bound.
A program may use at most 128 MiB of HBM per device.

v0:
```python
import jax
import jax.numpy as jnp
from jax import lax
from jax.sharding import PartitionSpec as P

HD = 64
POOL = 4


def padded(block, sides, width):
    for axis, dim in sides:
        count = lax.axis_size(axis)
        forward = [(i, i + 1) for i in range(count - 1)]
        backward = [(target, source) for source, target in forward]
        low = lax.ppermute(
            lax.slice_in_dim(block, block.shape[dim] - width, None, axis=dim), axis, forward
        )
        high = lax.ppermute(lax.slice_in_dim(block, 0, width, axis=dim), axis, backward)
        block = jnp.concatenate([low, block, high], axis=dim)
    return block


def product(form, left, right):
    return jnp.einsum(form, left, right, preferred_element_type=jnp.float32)


def project(rows, matrix):
    return jnp.dot(rows, matrix, preferred_element_type=jnp.float32)


def contract_rows(left, right):
    return lax.dot_general(
        left, right, (((0,), (0,)), ((), ())), preferred_element_type=jnp.float32
    )


def attend(inputs, weights):
    batch, count, width = inputs.shape
    heads = weights.shape[2] // HD
    flat_in = inputs.reshape(-1, width)
    queries = project(flat_in, weights[0]).astype(jnp.bfloat16).reshape(batch, count, heads, HD)
    key_rows = project(flat_in, weights[1]).astype(jnp.bfloat16).reshape(batch, count, heads, HD)
    value_rows = project(flat_in, weights[2]).astype(jnp.bfloat16).reshape(batch, count, heads, HD)
    scores = product("bqhd,bkhd->bhqk", queries, key_rows) * HD ** (-0.5)
    shifted = jnp.exp(scores - jnp.max(scores, axis=-1, keepdims=True))
    probs = shifted / jnp.sum(shifted, axis=-1, keepdims=True)
    probs_low = probs.astype(jnp.bfloat16)
    mixed = product("bhqk,bkhd->bqhd", probs_low, value_rows).astype(jnp.bfloat16)
    outputs = flat_in.astype(jnp.float32) + project(mixed.reshape(batch * count, -1), weights[3].T)
    return (
        outputs.reshape(batch, count, width).astype(jnp.bfloat16),
        (queries, key_rows, value_rows, probs, probs_low),
    )


def attend_back(cotangent, weights, saved):
    queries, key_rows, value_rows, probs, probs_low = saved
    batch, count, width = cotangent.shape
    heads = weights.shape[2] // HD
    flat_grad = cotangent.reshape(-1, width)
    grad_mixed = (
        project(flat_grad, weights[3]).astype(jnp.bfloat16).reshape(batch, count, heads, HD)
    )
    grad_probs = product("bqhd,bkhd->bhqk", grad_mixed, value_rows)
    grad_values = product("bhqk,bqhd->bkhd", probs_low, grad_mixed).astype(jnp.bfloat16)
    inner = jnp.sum(grad_probs * probs, axis=-1, keepdims=True)
    grad_scores = (probs * (grad_probs - inner) * HD ** (-0.5)).astype(jnp.bfloat16)
    grad_queries = product("bhqk,bkhd->bqhd", grad_scores, key_rows).astype(jnp.bfloat16)
    grad_keys = product("bhqk,bqhd->bkhd", grad_scores, queries).astype(jnp.bfloat16)
    total = flat_grad.astype(jnp.float32)
    total = total + project(grad_queries.reshape(batch * count, -1), weights[0].T)
    total = total + project(grad_keys.reshape(batch * count, -1), weights[1].T)
    total = total + project(grad_values.reshape(batch * count, -1), weights[2].T)
    return total.reshape(batch, count, width).astype(jnp.bfloat16)


def to_frames(tile_rows):
    return lax.all_to_all(tile_rows, ("row", "col"), split_axis=0, concat_axis=1, tiled=True)


def to_tiles(frame_rows):
    return lax.all_to_all(frame_rows, ("row", "col"), split_axis=1, concat_axis=0, tiled=True)


def with_border(field):
    return padded(field, (("row", 1), ("col", 2)), 1)


def shards(skip, w_up, w_in, w_out, spatial_w, temporal_w, grad_out):
    frames, tile_h, tile_w, chan = skip.shape
    wide = w_in.shape[1]
    coarse_h = tile_h // POOL
    coarse_w = tile_w // POOL
    local_tok = coarse_h * coarse_w
    blocks = skip.astype(jnp.float32).reshape(frames, coarse_h, POOL, coarse_w, POOL, chan)
    pooled_rows = (
        jnp.mean(blocks, axis=(2, 4)).astype(jnp.bfloat16).reshape(frames, local_tok, chan)
    )
    coarse = (
        project(pooled_rows.reshape(-1, chan), w_in)
        .astype(jnp.bfloat16)
        .reshape(frames, local_tok, wide)
    )
    coarse_rel = to_frames(coarse)
    attended_rel, saved_space = attend(coarse_rel, spatial_w)
    attended = to_tiles(attended_rel)
    timed_pixel, saved_time = attend(jnp.swapaxes(attended, 0, 1), temporal_w)
    timed = jnp.swapaxes(timed_pixel, 0, 1).reshape(frames * local_tok, wide)
    expanded = project(timed, w_out).reshape(frames, coarse_h, 1, coarse_w, 1, chan)
    united = (blocks + expanded).reshape(frames, tile_h, tile_w, chan).astype(jnp.bfloat16)
    united_pad = with_border(united)
    grad_pad = with_border(grad_out)
    grad_rows = grad_out.reshape(-1, chan)
    tap_grads = []
    grad_united = jnp.zeros((frames * tile_h * tile_w, chan), jnp.float32)
    for tap_row in range(3):
        for tap_col in range(3):
            tap = 3 * tap_row + tap_col
            shifted_in = united_pad[
                :, tap_row : tap_row + tile_h, tap_col : tap_col + tile_w, :
            ].reshape(-1, chan)
            tap_grads.append(contract_rows(shifted_in, grad_rows))
            shifted_grad = grad_pad[
                :, 2 - tap_row : 2 - tap_row + tile_h, 2 - tap_col : 2 - tap_col + tile_w, :
            ].reshape(-1, chan)
            grad_united = grad_united + project(shifted_grad, w_up[tap].T)
    grad_w_up = jnp.stack(tap_grads)
    grad_united = grad_united.astype(jnp.bfloat16).reshape(
        frames, coarse_h, POOL, coarse_w, POOL, chan
    )
    grad_expanded = (
        jnp.sum(grad_united.astype(jnp.float32), axis=(2, 4)).astype(jnp.bfloat16).reshape(-1, chan)
    )
    grad_timed = (
        project(grad_expanded, w_out.T).astype(jnp.bfloat16).reshape(frames, local_tok, wide)
    )
    grad_w_out = contract_rows(timed, grad_expanded)
    grad_att_pixel = attend_back(jnp.swapaxes(grad_timed, 0, 1), temporal_w, saved_time)
    grad_attended = jnp.swapaxes(grad_att_pixel, 0, 1)
    grad_att_rel = to_frames(grad_attended)
    grad_coarse_rel = attend_back(grad_att_rel, spatial_w, saved_space)
    grad_coarse = to_tiles(grad_coarse_rel).reshape(-1, wide)
    grad_pooled = project(grad_coarse, w_in.T).astype(jnp.bfloat16)
    grad_w_in = contract_rows(pooled_rows.reshape(-1, chan), grad_coarse)
    spread = grad_pooled.astype(jnp.float32).reshape(frames, coarse_h, 1, coarse_w, 1, chan) / (
        POOL * POOL
    )
    grad_skip = (
        (grad_united.astype(jnp.float32) + spread)
        .reshape(frames, tile_h, tile_w, chan)
        .astype(jnp.bfloat16)
    )
    final_up, final_in, final_out = lax.psum(
        (grad_w_up, grad_w_in, grad_w_out), ("row", "col", "grp")
    )
    return (grad_skip, final_up, final_in, final_out)


def solution(mesh):
    in_specs = (P("grp", "row", "col", None), P(), P(), P(), P(), P(), P("grp", "row", "col", None))
    out_specs = (P("grp", "row", "col", None), P(), P(), P())
    return jax.shard_map(shards, mesh=mesh, in_specs=in_specs, out_specs=out_specs, check_vma=False)
```

profile of v0, /device:TPU:1, one launch (start us, length us, event | category | flops | bytes accessed | tf_op | source)
XLA Modules:
  0.0 510.6 jit_solution(5264054183028924066)
XLA Ops:
  9.2 4.7 collective-permute-start
  19.4 12.2 %all-to-all-start = ((bf16[64,2,1280]{2,1,0:T(2,128)(2,1)}), bf16[64,2,1280]{2,1,0:T(2,128)(2,1)S(1)}, u32[]{:S(2)}, u32[]{:S(2)}) async-start(bf16[64,2,1280]{2,1,0:T(2,128)(2,1)} %reshape.278), calls=%async_computation | async-start | bytes 655360 | tf_op jit(solution)/shard_map/all_to_all | solution.py:78
  38.3 3.7 collective-permute-start.3
  46.0 3.4 pad_maximum_fusion.2
  49.3 3.7 reshape.266
  53.0 3.8 reshape.272
  56.8 3.8 fusion.149
  63.5 2.5 fusion.99
  66.0 2.5 fusion.102
  71.6 2.2 fusion.195
  73.8 2.2 convolution_convert_fusion.9
  76.0 2.1 fusion.11
  80.0 3.5 reduce.13
  84.4 11.6 %all-to-all-start.1 = ((bf16[64,2,1280]{2,1,0:T(2,128)(2,1)}), bf16[64,2,1280]{2,1,0:T(2,128)(2,1)}, u32[]{:S(2)}, u32[]{:S(2)}) async-start(bf16[64,2,1280]{2,1,0:T(2,128)(2,1)} %reshape.316), calls=%async_computation.1 | async-start | bytes 655360 | tf_op jit(solution)/shard_map/all_to_all | solution.py:82
  96.0 6.8 %pad_maximum_fusion.1 = (bf16[64,8,4,320]{3,0,2,1:T(8,128)(2,1)}, bf16[64,8,4,320]{3,0,2,1:T(8,128)(2,1)S(1)}, bf16[64,8,4,320]{3,0,2,1:T(8,128)(2,1)}, bf16[64,...) fusion(bf16[64,10,4,320]{3,0,2,1:T(8,128)(2,1)} %copy-done.15, ...), kind=kLoop, calls=%fused_computation.79 | loop fusion | flops 3932160 | bytes 10321920 | tf_op jit(solution)/shard_map/concatenate | solution.py:19
  102.9 2.4 copy.216
  105.2 3.7 reshape.267
  109.0 3.8 copy.214
  112.7 3.7 reshape.265
  116.5 3.9 fusion.151
  120.4 2.4 copy.217
  122.7 3.7 reshape.268
  126.5 3.8 copy.218
  130.2 3.7 reshape.270
  134.0 3.8 copy.219
  137.7 3.9 reshape.271
  141.6 3.8 copy.221
  145.4 3.7 reshape.273
  149.1 4.1 convolution_add_fusion.6
  162.3 2.5 copy.223
  164.9 3.9 reshape.274
  168.7 2.6 reduce_sum.64
  179.2 3.6 reshape.317
  182.8 3.7 bitcast_reduce_fusion.1
  189.4 2.6 fusion.111
  192.0 2.5 fusion.120
  194.6 2.5 fusion.114
  209.3 2.1 fusion.197
  211.4 2.3 fusion.196
  213.7 2.8 fusion.95
  216.6 2.9 fusion.96
  219.4 2.4 fusion.97
  221.8 2.5 fusion.98
  226.4 3.0 convolution_add_fusion.13
  232.8 2.3 convolution_add_fusion.12
  238.2 10.0 %all-to-all-start.2 = ((bf16[64,2,1280]{2,1,0:T(2,128)(2,1)}), bf16[64,2,1280]{2,1,0:T(2,128)(2,1)S(1)}, u32[]{:S(2)}, u32[]{:S(2)}) async-start(bf16[64,2,1280]{2,1,0:T(2,128)(2,1)} %bitcast.295), calls=%async_computation.2 | async-start | bytes 655360 | tf_op jit(solution)/shard_map/all_to_all | solution.py:78
  252.1 2.2 fusion.9
  256.8 4.0 collective-permute-start.4
  266.0 4.0 collective-permute-start.6
  274.8 2.1 convolution_convert_fusion.8
  276.9 2.1 convolution_convert_fusion.7
  281.0 2.1 convolution_add_fusion.9
  287.2 2.6 reduce.14
  290.6 14.2 %all-to-all-start.3 = ((bf16[64,2,1280]{2,1,0:T(2,128)(2,1)}), bf16[64,2,1280]{2,1,0:T(2,128)(2,1)S(1)}, u32[]{:S(2)}, u32[]{:S(2)}) async-start(bf16[64,2,1280]{2,1,0:T(2,128)(2,1)} %reshape.318), calls=%async_computation.3 | async-start | bytes 655360 | tf_op jit(solution)/shard_map/all_to_all | solution.py:82
  305.1 3.2 fusion.81
  310.1 2.7 fusion.80
  312.8 2.7 fusion.79
  317.3 2.7 fusion.78
  320.0 2.7 fusion.77
  324.4 2.8 fusion.76
  332.4 4.9 reshape.299
  338.3 3.9 add_convert_fusion
  342.2 153.4 %all-reduce.3.cloned.1.call-done = (f32[9,320,320]{2,1,0:T(8,128)}, f32[320,1280]{1,0:T(8,128)}, f32[1280,320]{0,1:T(8,128)}) async-done(((f32[9,320,320]{2,1,0:T(8,128)}, f32[320,1280]{1,0:T(8,128)}, f32[1280,320]{0,1:T(8,128)}), (f32[9,320,320]{2,1,0:T(8,128)}, f32[320,1280]{1,0:T(8,128)}, f32[1280,320]{0,1:T(8,128)})) %all-reduce.3.cloned.1.call-update) | async-done | bytes 6963216 | tf_op jit(solution)/shard_map/psum | solution.py:153
  495.6 4.7 copy.351
  (182 shorter events, 105.4 us)
Async XLA Ops:
  7.2 164.8 %copy-start = (bf16[1280,320]{0,1:T(8,128)(2,1)S(1)}, bf16[1280,320]{0,1:T(8,128)(2,1)}, u32[]{:S(2)}) copy-start(bf16[1280,320]{0,1:T(8,128)(2,1)} %param.10) | copy-start | bytes 2457604
  7.2 8.7 %copy-start.12 = (bf16[64,8,4,320]{3,2,1,0:T(4,128)(2,1)S(1)}, bf16[64,8,4,320]{3,2,1,0:T(4,128)(2,1)}, u32[]{:S(2)}) copy-start(bf16[64,8,4,320]{3,2,1,0:T(4,128)(2,1)} %param.7) | copy-start | bytes 3932164
  9.2 24.1 %collective-permute-start = (bf16[64,1,4,320]{3,0,2,1:T(8,128)(2,1)}, bf16[64,1,4,320]{3,0,2,1:T(8,128)(2,1)}, u32[]{:S(2)}, u32[]{:S(2)}) collective-permute-start(bf16[64,1,4,320]{3,0,2,1:T(8,128)(2,1)} %copy.329), channel_id=1, source_target_pairs={{0,16},{16,32},{32,48},{48,64},{64,80},{80,96},{96,112},{1,17},{17... | collective-permute-start | bytes 491528 | tf_op jit(solution)/shard_map/ppermute | solution.py:15
  13.9 3.4 copy-start.16
  14.6 20.4 %collective-permute-start.1 = (bf16[64,1,4,320]{3,0,2,1:T(8,128)(2,1)}, bf16[64,1,4,320]{3,0,2,1:T(8,128)(2,1)}, u32[]{:S(2)}, u32[]{:S(2)}) collective-permute-start(bf16[64,1,4,320]{3,0,2,1:T(8,128)(2,1)} %copy.330), channel_id=1, source_target_pairs={{16,0},{32,16},{48,32},{64,48},{80,64},{96,80},{112,96},{17,1},{33... | collective-permute-start | bytes 491528 | tf_op jit(solution)/shard_map/ppermute | solution.py:18
  16.4 15.2 %copy-start.2 = (bf16[64,8,4,320]{3,2,1,0:T(4,128)(2,1)S(1)}, bf16[64,8,4,320]{3,2,1,0:T(4,128)(2,1)}, u32[]{:S(2)}) copy-start(bf16[64,8,4,320]{3,2,1,0:T(4,128)(2,1)} %param.13) | copy-start | bytes 3932164
  19.4 41.2 %all-to-all-start = ((bf16[64,2,1280]{2,1,0:T(2,128)(2,1)}), bf16[64,2,1280]{2,1,0:T(2,128)(2,1)S(1)}, u32[]{:S(2)}, u32[]{:S(2)}) async-start(bf16[64,2,1280]{2,1,0:T(2,128)(2,1)} %reshape.278), calls=%async_computation | async-start | bytes 655360 | tf_op jit(solution)/shard_map/all_to_all | solution.py:78
  36.0 1.3 copy-start.15
  38.3 57.7 %collective-permute-start.3 = (bf16[64,10,1,320]{3,0,2,1:T(8,128)(2,1)}, bf16[64,10,1,320]{3,0,2,1:T(8,128)(2,1)}, u32[]{:S(2)}, u32[]{:S(2)}) collective-permute-start(bf16[64,10,1,320]{3,0,2,1:T(8,128)(2,1)} %get-tuple-element.19), channel_id=1, source_target_pairs={{0,2},{2,4},{4,6},{6,8},{8,10},{10,12},{12,14},{1,3},{3,5},{5,7},{... | collective-permute-start | bytes 1228808 | tf_op jit(solution)/shard_map/ppermute | solution.py:15
  42.0 54.0 %collective-permute-start.2 = (bf16[64,10,1,320]{3,0,2,1:T(8,128)(2,1)}, bf16[64,10,1,320]{3,0,2,1:T(8,128)(2,1)}, u32[]{:S(2)}, u32[]{:S(2)}) collective-permute-start(bf16[64,10,1,320]{3,0,2,1:T(8,128)(2,1)} %get-tuple-element.18), channel_id=1, source_target_pairs={{2,0},{4,2},{6,4},{8,6},{10,8},{12,10},{14,12},{3,1},{5,3},{7,5},{... | collective-permute-start | bytes 1228808 | tf_op jit(solution)/shard_map/ppermute | solution.py:18
  61.5 2.0 copy-start.29
  68.7 7.2 %copy-start.34 = (bf16[128,640]{0,1:T(8,128)(2,1)}, bf16[128,640]{0,1:T(8,128)(2,1)S(1)}, u32[]{:S(2)}) copy-start(bf16[128,640]{0,1:T(8,128)(2,1)S(1)} %copy.229) | copy-start | bytes 491524
  69.9 6.1 %copy-start.24 = (bf16[128,640]{0,1:T(8,128)(2,1)}, bf16[128,640]{0,1:T(8,128)(2,1)S(1)}, u32[]{:S(2)}) copy-start(bf16[128,640]{0,1:T(8,128)(2,1)S(1)} %copy.227) | copy-start | bytes 491524
  73.8 4.3 copy-start.38
  84.4 94.9 %all-to-all-start.1 = ((bf16[64,2,1280]{2,1,0:T(2,128)(2,1)}), bf16[64,2,1280]{2,1,0:T(2,128)(2,1)}, u32[]{:S(2)}, u32[]{:S(2)}) async-start(bf16[64,2,1280]{2,1,0:T(2,128)(2,1)} %reshape.316), calls=%async_computation.1 | async-start | bytes 655360 | tf_op jit(solution)/shard_map/all_to_all | solution.py:82
  116.5 3.9 copy-start.11
  149.1 4.2 copy-start.10
  149.1 4.2 copy-start.17
  153.3 1.4 copy-start.6
  154.7 1.4 copy-start.8
  156.1 1.4 copy-start.9
  157.6 1.4 copy-start.7
  159.0 1.4 copy-start.14
  171.3 0.6 copy-start.22
  174.2 0.7 copy-start.20
  189.4 5.2 %copy-start.27 = (bf16[2,64,1280]{2,1,0:T(8,128)(2,1)}, bf16[2,64,1280]{2,1,0:T(8,128)(2,1)S(1)}, u32[]{:S(2)}) copy-start(bf16[2,64,1280]{2,1,0:T(8,128)(2,1)S(1)} %copy.232) | copy-start | bytes 983044
  226.4 3.0 copy-start.28
  232.8 2.3 copy-start.26
  238.2 33.3 %all-to-all-start.2 = ((bf16[64,2,1280]{2,1,0:T(2,128)(2,1)}), bf16[64,2,1280]{2,1,0:T(2,128)(2,1)S(1)}, u32[]{:S(2)}, u32[]{:S(2)}) async-start(bf16[64,2,1280]{2,1,0:T(2,128)(2,1)} %bitcast.295), calls=%async_computation.2 | async-start | bytes 655360 | tf_op jit(solution)/shard_map/all_to_all | solution.py:78
  252.1 2.7 copy-start.13
  254.9 6.0 %copy-start.23 = (bf16[64,2,320]{2,1,0:T(2,128)(2,1)S(1)}, bf16[64,2,320]{2,1,0:T(2,128)(2,1)}, u32[]{:S(2)}) copy-start(bf16[64,2,320]{2,1,0:T(2,128)(2,1)} %copy-done.22) | copy-start | bytes 245764
  255.5 10.5 %copy-start.3 = (bf16[64,8,4,320]{3,0,2,1:T(8,128)(2,1)}, bf16[64,8,4,320]{3,0,2,1:T(8,128)(2,1)S(1)}, u32[]{:S(2)}) copy-start(bf16[64,8,4,320]{3,0,2,1:T(8,128)(2,1)S(1)} %fusion.4) | copy-start | bytes 3932164
  255.5 6.9 %collective-permute-start.5 = (bf16[64,1,4,320]{3,0,2,1:T(8,128)(2,1)S(1)}, bf16[64,1,4,320]{3,0,2,1:T(8,128)(2,1)S(1)}, u32[]{:S(2)}, u32[]{:S(2)}) collective-permute-start(bf16[64,1,4,320]{3,0,2,1:T(8,128)(2,1)S(1)} %get-tuple-element.21), channel_id=1, source_target_pairs={{16,0},{32,16},{48,32},{64,48},{80,64},{96,80},{112,96},{17,1},{33... | collective-permute-start | bytes 491528 | tf_op jit(solution)/shard_map/ppermute | solution.py:18
  256.8 7.3 %collective-permute-start.4 = (bf16[64,1,4,320]{3,0,2,1:T(8,128)(2,1)S(1)}, bf16[64,1,4,320]{3,0,2,1:T(8,128)(2,1)S(1)}, u32[]{:S(2)}, u32[]{:S(2)}) collective-permute-start(bf16[64,1,4,320]{3,0,2,1:T(8,128)(2,1)S(1)} %get-tuple-element.20), channel_id=1, source_target_pairs={{0,16},{16,32},{32,48},{48,64},{64,80},{80,96},{96,112},{1,17},{17... | collective-permute-start | bytes 491528 | tf_op jit(solution)/shard_map/ppermute | solution.py:15
  262.4 9.0 %copy-start.30 = (bf16[64,1,4,320]{3,0,2,1:T(8,128)(2,1)}, bf16[64,1,4,320]{3,0,2,1:T(8,128)(2,1)S(1)}, u32[]{:S(2)}) copy-start(bf16[64,1,4,320]{3,0,2,1:T(8,128)(2,1)S(1)} %collective-permute-done.5) | copy-start | bytes 491524
  264.2 0.7 copy-start.32
  266.0 7.6 %copy-start.25 = (bf16[128,640]{0,1:T(8,128)(2,1)S(1)}, bf16[128,640]{0,1:T(8,128)(2,1)}, u32[]{:S(2)}) copy-start(bf16[128,640]{0,1:T(8,128)(2,1)} %copy-done.24) | copy-start | bytes 491524
  266.0 39.1 %collective-permute-start.6 = (bf16[64,10,1,320]{3,0,2,1:T(8,128)(2,1)}, bf16[64,10,1,320]{3,0,2,1:T(8,128)(2,1)}, u32[]{:S(2)}, u32[]{:S(2)}) collective-permute-start(bf16[64,10,1,320]{3,0,2,1:T(8,128)(2,1)} %get-tuple-element.14), channel_id=1, source_target_pairs={{0,2},{2,4},{4,6},{6,8},{8,10},{10,12},{12,14},{1,3},{3,5},{5,7},{... | collective-permute-start | bytes 1228808 | tf_op jit(solution)/shard_map/ppermute | solution.py:15
  270.0 4.8 copy-start.35
  270.0 4.8 copy-start.39
  270.0 40.1 %collective-permute-start.7 = (bf16[64,10,1,320]{3,0,2,1:T(8,128)(2,1)}, bf16[64,10,1,320]{3,0,2,1:T(8,128)(2,1)}, u32[]{:S(2)}, u32[]{:S(2)}) collective-permute-start(bf16[64,10,1,320]{3,0,2,1:T(8,128)(2,1)} %get-tuple-element.13), channel_id=1, source_target_pairs={{2,0},{4,2},{6,4},{8,6},{10,8},{12,10},{14,12},{3,1},{5,3},{7,5},{... | collective-permute-start | bytes 1228808 | tf_op jit(solution)/shard_map/ppermute | solution.py:18
  273.5 3.4 copy-start.37
  281.0 2.1 copy-start.36
  290.6 36.6 %all-to-all-start.3 = ((bf16[64,2,1280]{2,1,0:T(2,128)(2,1)}), bf16[64,2,1280]{2,1,0:T(2,128)(2,1)S(1)}, u32[]{:S(2)}, u32[]{:S(2)}) async-start(bf16[64,2,1280]{2,1,0:T(2,128)(2,1)} %reshape.318), calls=%async_computation.3 | async-start | bytes 655360 | tf_op jit(solution)/shard_map/all_to_all | solution.py:82
  304.8 3.5 copy-start.33
  304.8 190.7 %all-reduce.3.cloned.1.call-start = ((), (), s32[]{:S(2)}) async-start(), calls=%async_computation.4 | async-start | bytes 15400960 | tf_op jit(solution)/shard_map/psum | solution.py:153
  305.1 3.2 copy-start.4
  308.3 1.7 copy-start.31
  324.4 3.0 copy-start.21
  329.0 1.3 copy-start.5
  495.6 4.8 copy-start.19
  500.3 2.0 copy-start.18
  500.3 3.2 copy-start.1
Sparse Core Ops, SparseCore 0:
  329.2 166.3 all-reduce.2
where the time goes:
time: 518 us; the launch traced here: 511 us
  waiting for transfers between devices  155 us (30%)
  local copies, waits for them, and re-layouts  136 us (26%)
  matrix products  109 us (21%)
  starting transfers between devices  70.4 us (14%)
  other arithmetic  25 us (5%)
  between operations  15 us (3%)
    psum x1, waiting for transfers between devices, shards(): lax.psum((grad_w_up, grad_w_in, grad_w_out), ('row', 'col', 'grp'))  153 us
    dot_general x29, matrix products, project(): return jnp.dot(rows, matrix, preferred_element_type=jnp.float32)  57.5 us
    reshape x9, local copies, waits for them, and re-layouts, shards(): shifted_grad = grad_pad[:, 2 - tap_row:2 - tap_row + tile_h, 2 - tap_col:...  31.8 us
    all_to_all x2, starting transfers between devices, to_tiles(): lax.all_to_all(frame_rows, ('row', 'col'), split_axis=1, concat_axis=0, t...  25.9 us
    dot_general x11, matrix products, contract_rows(): lax.dot_general(left, right, (((0,), (0,)), ((), ())), preferred_element_...  25.2 us
    unnamed x92, local copies, waits for them, and re-layouts  24.4 us
    all_to_all x2, starting transfers between devices, to_frames(): lax.all_to_all(tile_rows, ('row', 'col'), split_axis=0, concat_axis=1, ti...  22.2 us
    dot_general x10, matrix products, product(): return jnp.einsum(form, left, right, preferred_element_type=jnp.float32)  21.6 us
  transfers between devices with their start and end apart: 13, of which 2 were waited for; matrix products, arithmetic and copies ran while one was open for 38% of the time, Pallas kernels for 0%

commit v1 on v0

v1 whole, which is shorter than its diff:
```python
import jax
import jax.numpy as jnp
from jax import lax
from jax.experimental import pallas as pl
from jax.experimental.pallas import tpu as pltpu
from jax.sharding import PartitionSpec as P

HD = 64
POOL = 4
N = 8
F32 = jnp.float32
BF = jnp.bfloat16
MESH = pl.DeviceIdType.MESH


def dot(a, b):
    return lax.dot_general(a, b, (((1,), (0,)), ((), ())), preferred_element_type=F32)


def dot_nt(a, b):
    return lax.dot_general(a, b, (((1,), (1,)), ((), ())), preferred_element_type=F32)


def dot_tn(a, b):
    return lax.dot_general(a, b, (((0,), (0,)), ((), ())), preferred_element_type=F32)


def permutation(back):
    to = lax.broadcasted_iota(jnp.int32, (128, 128), 1 if back else 0)
    fro = lax.broadcasted_iota(jnp.int32, (128, 128), 0 if back else 1)
    wanted = (to % 16 // 2) * 16 + (to % 2) * 8 + to // 16
    return jnp.where(fro == wanted, 1.0, 0.0).astype(BF)


def halves():
    lane = lax.broadcasted_iota(jnp.int32, (128, 128), 1)
    low = jnp.where(lane < HD, 1.0, 0.0)
    return low.astype(BF), (1.0 - low).astype(BF), lane < HD


def lanes(pair):
    return pl.ds(pl.multiple_of(pair * 128, 128), 128)


def attend(q, k, v, probs, mixed, same_set):
    low, high, is_low = halves()

    def pair_step(pair, carry):
        cols = lanes(pair)
        q2, k2, v2 = q[:, cols], k[:, cols], v[:, cols]
        stacked = jnp.concatenate([q2 * low, q2 * high], axis=0)
        scores = dot_nt(stacked, k2) * (HD ** -0.5)
        if same_set is not None:
            scores = jnp.where(same_set, scores, -3e38)
        shifted = jnp.exp(scores - jnp.max(scores, axis=-1, keepdims=True))
        prob = shifted / jnp.sum(shifted, axis=-1, keepdims=True)
        probs[pair] = prob
        out = dot(prob.astype(BF), v2)
        mixed[:, cols] = jnp.where(is_low, out[:128], out[128:]).astype(BF)
        return carry

    lax.fori_loop(0, q.shape[1] // 128, pair_step, 0)


def attend_back(q, k, v, probs, gmix, gq, gk, gv):
    low, high, is_low = halves()

    def pair_step(pair, carry):
        cols = lanes(pair)
        q2, k2, v2, g2 = q[:, cols], k[:, cols], v[:, cols], gmix[:, cols]
        stacked = jnp.concatenate([q2 * low, q2 * high], axis=0)
        gstacked = jnp.concatenate([g2 * low, g2 * high], axis=0)
        prob = probs[pair]
        gprob = dot_nt(gstacked, v2)
        inner = jnp.sum(gprob * prob, axis=-1, keepdims=True)
        gscore = prob * (gprob - inner) * (HD ** -0.5)
        gv[:, cols] = dot_tn(prob.astype(BF), gstacked).astype(BF)
        gscore = gscore.astype(BF)
        out = dot(gscore, k2)
        gq[:, cols] = jnp.where(is_low, out[:128], out[128:]).astype(BF)
        gk[:, cols] = dot_tn(gscore, stacked).astype(BF)
        return carry

    lax.fori_loop(0, q.shape[1] // 128, pair_step, 0)


def wide_nt(base, pairs, out):
    def step(at, carry):
        cols = pl.ds(pl.multiple_of(at * 256, 256), 256)
        total = base[:, cols].astype(F32)
        for x, matrix, index in pairs:
            total = total + dot_nt(x[...], matrix[index, cols, :])
        out[:, cols] = total.astype(BF)
        return carry

    lax.fori_loop(0, out.shape[1] // 256, step, 0)


def main_kernel(
    skip_hbm, grad_hbm, wup_hbm, win_hbm, wout_hbm, sw_hbm, tw_hbm,
    out, gup, gin, gout,
    skip, gpad, wup, win, wout, sw, tw,
    a1s, a1r, a2s, a2r, b1s, b1r, b2s, b2r, c1s, c1r, c2s, c2r, d1s, d1r, d2s, d2r,
    pooled_t, coarse_t, pooled_f, coarse_f, gunited, gexp, gexp_t, gtimed, gcoarse,
    qs, ks, vs, probs_s, qt, kt, vt, probs_t, mix, mix_t, attended, timed, gmix, gq, gk, gv, gatt,
    unit_t,
    load_sem, halo_sem, swap_sem,
):
    r, c, g = lax.axis_index("row"), lax.axis_index("col"), lax.axis_index("grp")
    loads = {}
    for at, (name, src, dst) in enumerate((
        ("grad", grad_hbm, gpad.at[1:9, 1:5]),
        ("skip", skip_hbm, skip),
        ("win", win_hbm, win),
        ("wup", wup_hbm, wup),
        ("wout", wout_hbm, wout),
        ("sw", sw_hbm, sw),
        ("tw", tw_hbm, tw),
    )):
        loads[name] = pltpu.make_async_copy(src, dst, load_sem.at[at])
        loads[name].start()

    around = [(dr, dc) for dr in (-1, 0, 1) for dc in (-1, 0, 1) if (dr, dc) != (0, 0)]

    def beside(dr, dc):
        return {"row": (r + dr + N) % N, "col": (c + dc + N) % N}

    barrier = pltpu.get_barrier_semaphore()
    for d in range(1, N):
        pl.semaphore_signal(barrier, 1, device_id={"row": (r + d) % N}, device_id_type=MESH)
        pl.semaphore_signal(barrier, 1, device_id={"col": (c + d) % N}, device_id_type=MESH)
    for dr, dc in around:
        if dr != 0 and dc != 0:
            pl.semaphore_signal(barrier, 1, device_id=beside(dr, dc), device_id_type=MESH)
    pl.semaphore_wait(barrier, 2 * (N - 1) + 4)

    def send(stage, src, dst, axis, me):
        dst[me] = src[me]

        def step(d, carry):
            peer = (me + d) % N
            pltpu.make_async_remote_copy(
                src.at[peer], dst.at[me], swap_sem.at[stage, 0, peer], swap_sem.at[stage, 1, me],
                device_id={axis: peer}, device_id_type=MESH,
            ).start()
            return carry

        lax.fori_loop(1, N, step, 0)

    def arrive(stage, src, dst, axis, me):
        def step(d, carry):
            peer = (me + d) % N
            pltpu.make_async_remote_copy(
                src.at[peer], dst.at[peer], swap_sem.at[stage, 0, peer], swap_sem.at[stage, 1, peer],
                device_id={axis: peer}, device_id_type=MESH,
            ).wait()
            return carry

        lax.fori_loop(1, N, step, 0)

    def turn(src, dst, back):
        width = src.shape[2]
        rows = src[...].reshape(128, width)
        dst[...] = dot(permutation(back), rows).astype(BF).reshape(N, 16, width)

    def halo(k):
        dr, dc = around[k]
        src = gpad.at[
            {-1: pl.ds(1, 1), 0: pl.ds(1, 8), 1: pl.ds(8, 1)}[dr],
            {-1: pl.ds(1, 1), 0: pl.ds(1, 4), 1: pl.ds(4, 1)}[dc],
        ]
        dst = gpad.at[
            {-1: pl.ds(9, 1), 0: pl.ds(1, 8), 1: pl.ds(0, 1)}[dr],
            {-1: pl.ds(5, 1), 0: pl.ds(1, 4), 1: pl.ds(0, 1)}[dc],
        ]
        return pltpu.make_async_remote_copy(
            src, dst, halo_sem.at[0, k], halo_sem.at[1, k],
            device_id=beside(dr, dc), device_id_type=MESH,
        )

    loads["grad"].wait()
    for k in range(8):
        halo(k).start()

    loads["skip"].wait()
    means = []
    for p in range(2):
        total = jnp.zeros(skip.shape[2:], F32)
        for i in range(POOL):
            for j in range(POOL):
                total = total + skip[p * POOL + i, j].astype(F32)
        means.append(total * (1.0 / (POOL * POOL)))
    for f in range(N):
        rows = jnp.concatenate([means[0][8 * f:8 * f + 8], means[1][8 * f:8 * f + 8]], axis=0)
        a1s[f] = rows.astype(BF)
    pooled_t[...] = a1s[...].reshape(128, -1)
    send(0, a1s, a1r, "row", r)

    loads["win"].wait()
    coarse_t[...] = dot(pooled_t[...], win[...]).astype(BF)
    loads["wup"].wait()
    for k in range(8):
        halo(k).wait()

    @pl.when(r == 0)
    def _():
        gpad[0] = jnp.zeros(gpad.shape[1:], BF)

    @pl.when(r == N - 1)
    def _():
        gpad[9] = jnp.zeros(gpad.shape[1:], BF)

    @pl.when(c == 0)
    def _():
        gpad[:, 0] = jnp.zeros((10,) + gpad.shape[2:], BF)

    @pl.when(c == N - 1)
    def _():
        gpad[:, 5] = jnp.zeros((10,) + gpad.shape[2:], BF)

    chan = gpad.shape[3]
    gexp[...] = jnp.zeros_like(gexp)

    def back_rows(first, last):
        def step(i, carry):
            total = jnp.zeros((256, chan), F32)
            for dy in range(3):
                for dx in range(3):
                    rows = gpad[i + 2 - dy, pl.ds(2 - dx, 4)].reshape(256, chan)
                    total = total + dot_nt(rows, wup[3 * dy + dx])
            low = total.astype(BF)
            gunited[i] = low.reshape(4, 64, chan)
            gexp[i // POOL] += jnp.sum(low.astype(F32).reshape(4, 64, chan), axis=0)
            return carry

        lax.fori_loop(first, last, step, 0)

    back_rows(0, 3)
    arrive(0, a1s, a1r, "row", r)
    turn(a1r, a2s, False)
    send(1, a2s, a2r, "col", c)
    back_rows(3, 6)
    arrive(1, a2s, a2r, "col", c)
    pooled_f[...] = a2r[...].reshape(128, chan)

    coarse_f[...] = dot(pooled_f[...], win[...]).astype(BF)
    loads["sw"].wait()
    for m, ref in enumerate((qs, ks, vs)):
        ref[...] = dot(coarse_f[...], sw[m]).astype(BF)
    attend(qs, ks, vs, probs_s, mix, None)
    b1s[...] = mix[...].reshape(b1s.shape)
    send(2, b1s, b1r, "col", c)
    back_rows(6, 8)
    arrive(2, b1s, b1r, "col", c)
    turn(b1r, b2s, True)
    send(3, b2s, b2r, "row", r)
    loads["wout"].wait()
    loads["tw"].wait()
    for f in range(N):
        rows = jnp.concatenate([gexp[0, 8 * f:8 * f + 8], gexp[1, 8 * f:8 * f + 8]], axis=0)
        gexp_t[16 * f:16 * f + 16] = rows.astype(BF)
    gtimed[...] = dot(gexp_t[...], wout[...]).astype(BF)
    gmix[...] = dot(gtimed[...], tw[3]).astype(BF)
    arrive(3, b2s, b2r, "row", r)
    mix_t[...] = b2r[...].reshape(mix_t.shape)

    wide_nt(coarse_t, [(mix_t, sw, 3)], attended)
    for m, ref in enumerate((qt, kt, vt)):
        ref[...] = dot(attended[...], tw[m]).astype(BF)
    row_pixel = lax.broadcasted_iota(jnp.int32, (256, 128), 0) % 16 // 8
    key_pixel = lax.broadcasted_iota(jnp.int32, (256, 128), 1) % 16 // 8
    attend(qt, kt, vt, probs_t, mix, row_pixel == key_pixel)
    attend_back(qt, kt, vt, probs_t, gmix, gq, gk, gv)
    wide_nt(gtimed, [(gq, tw, 0), (gk, tw, 1), (gv, tw, 2)], gatt)
    c1s[...] = gatt[...].reshape(c1s.shape)
    send(4, c1s, c1r, "row", r)

    wide_nt(attended, [(mix, tw, 3)], timed)
    gout[...] = dot_tn(gexp_t[...], timed[...])
    expanded = dot_nt(timed[...], wout[...])
    for p in range(2):
        rows = jnp.concatenate(
            [expanded[16 * f + 8 * p:16 * f + 8 * p + 8] for f in range(N)], axis=0
        )

        def unite(i, carry):
            united = (skip[i].astype(F32) + rows[None]).astype(BF).reshape(256, chan)
            unit_t[:, pl.ds(pl.multiple_of(i * 256, 256), 256)] = united.T
            return carry

        lax.fori_loop(p * POOL, p * POOL + POOL, unite, 0)
    arrive(4, c1s, c1r, "row", r)
    turn(c1r, c2s, False)
    send(5, c2s, c2r, "col", c)

    def tap_step(tap, carry):
        dy, dx = tap // 3, tap % 3
        rows = gpad[pl.ds(2 - dy, 8), pl.ds(2 - dx, 4)].reshape(2048, chan)
        gup[tap] = dot(unit_t[...], rows)
        return carry

    lax.fori_loop(0, 9, tap_step, 0)
    arrive(5, c2s, c2r, "col", c)
    gatt[...] = c2r[...].reshape(gatt.shape)

    gmix[...] = dot(gatt[...], sw[3]).astype(BF)
    attend_back(qs, ks, vs, probs_s, gmix, gq, gk, gv)
    wide_nt(gatt, [(gq, sw, 0), (gk, sw, 1), (gv, sw, 2)], gcoarse)
    d1s[...] = dot_nt(gcoarse[...], win[...]).astype(BF).reshape(d1s.shape)
    send(6, d1s, d1r, "col", c)
    gin[...] = dot_tn(pooled_f[...], gcoarse[...])
    arrive(6, d1s, d1r, "col", c)
    turn(d1r, d2s, True)
    send(7, d2s, d2r, "row", r)
    arrive(7, d2s, d2r, "row", r)
    spread = d2r[...].reshape(128, chan).astype(F32) * (1.0 / (POOL * POOL))
    for p in range(2):
        rows = jnp.concatenate(
            [spread[16 * f + 8 * p:16 * f + 8 * p + 8] for f in range(N)], axis=0
        )

        def finish(i, carry):
            out[i] = (gunited[i].astype(F32) + rows[None]).astype(BF)
            return carry

        lax.fori_loop(p * POOL, p * POOL + POOL, finish, 0)


def shards(skip, w_up, w_in, w_out, spatial_w, temporal_w, grad_out):
    frames, tile_h, tile_w, chan = skip.shape
    wide = w_in.shape[1]
    att = spatial_w.shape[2]
    skip_t = jnp.transpose(skip, (1, 2, 0, 3))
    grad_t = jnp.transpose(grad_out, (1, 2, 0, 3))
    w_out_t = w_out.T

    def vm(shape, dtype=BF):
        return pltpu.VMEM(shape, dtype)

    tok = 128
    swaps = []
    for width in (chan, att, wide, chan):
        swaps += [vm((N, 16, width))] * 4
    scratch = [
        vm(skip_t.shape), vm((tile_h + 2, tile_w + 2, frames, chan)), vm(w_up.shape),
        vm(w_in.shape), vm(w_out_t.shape), vm(spatial_w.shape), vm(temporal_w.shape),
        *swaps,
        vm((tok, chan)), vm((tok, wide)), vm((tok, chan)), vm((tok, wide)),
        vm(skip_t.shape), vm((2, frames, chan), F32), vm((tok, chan)), vm((tok, wide)),
        vm((tok, wide)),
        vm((tok, att)), vm((tok, att)), vm((tok, att)), vm((att // 128, 256, 128), F32),
        vm((tok, att)), vm((tok, att)), vm((tok, att)), vm((att // 128, 256, 128), F32),
        vm((tok, att)), vm((tok, att)), vm((tok, wide)), vm((tok, wide)),
        vm((tok, att)), vm((tok, att)), vm((tok, att)), vm((tok, att)), vm((tok, wide)),
        vm((chan, frames * tile_h * tile_w)),
        pltpu.SemaphoreType.DMA((7,)), pltpu.SemaphoreType.DMA((2, 8)),
        pltpu.SemaphoreType.DMA((8, 2, N)),
    ]
    grad_skip, grad_w_up, grad_w_in, grad_w_out = pl.pallas_call(
        main_kernel,
        out_shape=(
            jax.ShapeDtypeStruct(skip_t.shape, BF),
            jax.ShapeDtypeStruct(w_up.shape, F32),
            jax.ShapeDtypeStruct(w_in.shape, F32),
            jax.ShapeDtypeStruct(w_out_t.shape, F32),
        ),
        in_specs=[pl.BlockSpec(memory_space=pl.ANY)] * 7,
        out_specs=[pl.BlockSpec(memory_space=pltpu.VMEM)] * 4,
        scratch_shapes=scratch,
        compiler_params=pltpu.CompilerParams(
            collective_id=0, has_side_effects=True, vmem_limit_bytes=60 * 1024 * 1024
        ),
        name="backward",
    )(skip_t, grad_t, w_up, w_in, w_out_t, spatial_w, temporal_w)
    grads = lax.psum((grad_w_up, grad_w_in, grad_w_out), ("row", "col", "grp"))
    return (jnp.transpose(grad_skip, (2, 0, 1, 3)), grads[0], grads[1], grads[2].T)


def solution(mesh):
    in_specs = (P("grp", "row", "col", None), P(), P(), P(), P(), P(), P("grp", "row", "col", None))
    out_specs = (P("grp", "row", "col", None), P(), P(), P())
    return jax.shard_map(shards, mesh=mesh, in_specs=in_specs, out_specs=out_specs, check_vma=False)
```

time: 518 us -> 283 us (0.55); the launches traced: 511 us -> 282 us
  local copies, waits for them, and re-layouts: 136 us -> 16.3 us
  matrix products: 109 us -> 0 us
  Pallas kernels: 0 us -> 90.9 us
  starting transfers between devices: 70.4 us -> 0.04 us
  other arithmetic: 25 us -> 0 us
  waiting for transfers between devices: 155 us -> 161 us
    dot_general x50 -> x0, matrix products: 104 us -> none  [the longest x29 57.5 us: project(): return jnp.dot(rows, matrix, preferred_element_type=jnp.float32)]
    pallas_call x0 -> x1, Pallas kernels: none -> 90.9 us  [shards(): pl.pallas_call(main_kernel, out_shape=(jax.ShapeDtypeStruct(skip_t.shape,...]
    reshape x27 -> x0, local copies, waits for them, and re-layouts: 57.7 us -> none  [the longest x9 31.8 us: shards(): shifted_grad = grad_pad[:, 2 - tap_row:2 - tap_row + tile_h, 2 - tap_col:...]
    all_to_all x4 -> x0, starting transfers between devices: 48 us -> none  [the longest x2 25.9 us: to_tiles(): lax.all_to_all(frame_rows, ('row', 'col'), split_axis=1, concat_axis=0, t...]
    slice x9 -> x0, local copies, waits for them, and re-layouts: 22.2 us -> none  [the longest x6 19.8 us: shards(): grad_pad[:, 2 - tap_row:2 - tap_row + tile_h, 2 - tap_col:2 - tap_col + t...]
    ppermute x8 -> x0, starting transfers between devices: 22.1 us -> none  [the longest x4 16.4 us: padded(): lax.ppermute(lax.slice_in_dim(block, block.shape[dim] - width, None, axis...]
    convert_element_type x16 -> x0, local copies, waits for them, and re-layouts: 21.4 us -> none  [the longest x2 6.91 us: shards(): grad_united.astype(jnp.float32) + spread]
    unnamed x92 -> x10, local copies, waits for them, and re-layouts: 24.4 us -> 11.7 us
  transfers between devices with their start and end apart: 13 -> 1, of which waited for: 2 -> 1; matrix products, arithmetic and copies ran while one was open for 38% -> 1% of each run, Pallas kernels for 0% -> 0%
where the time goes in v1:
time: 283 us; the launch traced here: 282 us
  waiting for transfers between devices  161 us (57%)
  Pallas kernels  90.9 us (32%)
  local copies, waits for them, and re-layouts  16.3 us (6%)
  between operations  14 us (5%)
    psum x1, waiting for transfers between devices, shards(): grads = lax.psum((grad_w_up, grad_w_in, grad_w_out), ('row', 'col', 'grp'))  161 us
    pallas_call x1, Pallas kernels, shards(): pl.pallas_call(main_kernel, out_shape=(jax.ShapeDtypeStruct(skip_t.shape,...  90.9 us
    unnamed x10, local copies, waits for them, and re-layouts  11.7 us
  transfers between devices with their start and end apart: 1, of which 1 were waited for; matrix products, arithmetic and copies ran while one was open for 1% of the time, Pallas kernels for 0%

profile of v1, /device:TPU:1, one launch (start us, length us, event | category | flops | bytes accessed | tf_op | source)
XLA Modules:
  0.0 282.4 jit_solution(5259836439384346429)
XLA Ops:
  7.2 0.0 all-reduce.3.cloned.1.call-start
  7.2 4.7 %copy_bitcast_fusion = (bf16[8,4,64,320]{3,2,1,0:T(8,128)(2,1)}, bf16[8,4,64,320]{3,2,1,0:T(8,128)(2,1)}) fusion(bf16[64,8,4,320]{3,2,1,0:T(4,128)(2,1)} %param.13, bf16[64,8,4,320]{3,2,1,0:T(4,128)(2,1)} %param.7), kind=kLoop, calls=%fused_computation | loop fusion | bytes 5242880 | tf_op jit(solution)/shard_map/transpose | solution.py:334
  11.9 90.9 %backward.1 = (bf16[8,4,64,320]{3,2,1,0:T(8,128)(2,1)}, f32[9,320,320]{2,1,0:T(8,128)}, f32[320,1280]{1,0:T(8,128)}, f32[320,1280]{1,0:T(8,128)}) custom-call(bf16[8,4,64,320]{3,2,1,0:T(8,128)(2,1)} %get-tuple-element.20.skip_hbm, bf16[8,4,64,320]{3,2,1,0:T(8,128)(2,1)} %get-tuple-element.19.grad_hbm, bf16[9,320,320]{2,1,0:T(8,128)(2,1)} %wup_hbm.1, ...), custom_call_target="tpu_custom_call" | custom-call | tf_op jit(solution)/shard_map/backward/pallas_call | solution.py:359
  102.8 0.0 copy-start.2
  102.8 0.0 all-reduce.3.cloned.1.call-update
  102.8 1.4 copy-done.2
  104.2 2.4 copy.13
  106.6 161.1 %all-reduce.3.cloned.1.call-done = (f32[9,320,320]{2,1,0:T(8,128)}, f32[320,1280]{1,0:T(8,128)}, f32[1280,320]{0,1:T(8,128)}) async-done(((f32[9,320,320]{2,1,0:T(8,128)}, f32[320,1280]{1,0:T(8,128)}, f32[1280,320]{0,1:T(8,128)}), (f32[9,320,320]{2,1,0:T(8,128)}, f32[320,1280]{1,0:T(8,128)}, f32[1280,320]{0,1:T(8,128)})) %all-reduce.3.cloned.1.call-update) | async-done | bytes 6963216 | tf_op jit(solution)/shard_map/psum | solution.py:375
  267.6 0.0 copy-start.1
  267.6 4.7 %copy.22 = f32[9,320,320]{2,1,0:T(8,128)} copy(f32[9,320,320]{2,1,0:T(8,128)} %get-tuple-element.26) | data formatting | bytes 7372800
  272.4 0.0 copy-done.1
  272.4 0.0 copy-start
  272.4 1.2 copy.23
  273.6 0.9 copy-done
  274.4 1.2 copy.24
Async XLA Ops:
  7.2 260.5 %all-reduce.3.cloned.1.call-start = ((), (), s32[]{:S(2)}) async-start(), calls=%async_computation | async-start | bytes 15400960 | tf_op jit(solution)/shard_map/psum | solution.py:375
  102.8 1.4 copy-start.2
  267.6 4.8 %copy-start.1 = (f32[320,1280]{1,0:T(8,128)S(1)}, f32[320,1280]{1,0:T(8,128)}, u32[]{:S(2)}) copy-start(f32[320,1280]{1,0:T(8,128)} %get-tuple-element.27) | copy-start | bytes 4915204
  272.4 2.0 copy-start
Sparse Core Ops, SparseCore 0:
  102.9 164.6 all-reduce.2

commit v2 on v1

--- a/solution.py
+++ b/solution.py
@@ -96,15 +96,168 @@
     lax.fori_loop(0, out.shape[1] // 256, step, 0)
 
 
+class Sum:
+    def __init__(self, place, g, blocks, paired, slots, part, slots2, own, slots3, row, fin, ring, pair):
+        self.place, self.g = place, g
+        self.blocks, self.paired, self.slots, self.part = blocks, paired, slots, part
+        self.slots2, self.own, self.slots3, self.row, self.fin = slots2, own, slots3, row, fin
+        self.ring, self.pair = ring, pair
+        self.u = blocks.shape[1] // 48
+
+    def me(self, k, stage):
+        return self.place[(k + stage) % 3]
+
+    def peer(self, k, stage, at):
+        x, y, z = self.place
+        axis = (k + stage) % 3
+        if axis == 0:
+            return {"row": at * 2 + y % 2}
+        if axis == 1:
+            return {"row": x * 2 + at % 2, "col": (at // 2) * 4 + z}
+        return {"col": (y // 2) * 4 + at}
+
+    def copy(self, src, dst, sem, k, stage, slot_s, slot_r, at):
+        return pltpu.make_async_remote_copy(
+            src, dst, self.ring.at[sem, 0, k, slot_s], self.ring.at[sem, 1, k, slot_r],
+            device_id=self.peer(k, stage, at), device_id_type=MESH,
+        )
+
+    def others(self, stage, step):
+        for k in range(3):
+            me = self.me(k, stage)
+
+            def one(d, carry):
+                step(k, me, (me + d) % 4)
+                return carry
+
+            lax.fori_loop(1, 4, one, 0)
+
+    def pair_copy(self):
+        return pltpu.make_async_remote_copy(
+            self.blocks.at[1 - self.g], self.paired, self.pair.at[0, 12], self.pair.at[1, 12],
+            device_id={"grp": 1 - self.g}, device_id_type=MESH,
+        )
+
+    def pair_send(self):
+        self.pair_copy().start()
+
+    def pair_add(self):
+        self.pair_copy().wait()
+        size = 4 * self.u
+
+        def step(at, carry):
+            some = pl.ds(at * size, size)
+            total = self.blocks[self.g, some].astype(F32) + self.paired[some].astype(F32)
+            self.paired[some] = total.astype(BF)
+            return carry
+
+        lax.fori_loop(0, 12, step, 0)
+
+    def spread_copy(self, stage, k, me, at, arriving):
+        if stage == 0:
+            size = 4 * self.u
+            src = self.paired.at[pl.ds((4 * k + at) * size, size)]
+            slots = self.slots
+        else:
+            src = self.part.at[k, pl.ds(at * self.u, self.u)]
+            slots = self.slots2
+        slot = at if arriving else me
+        return self.copy(src, slots.at[k, slot], stage, k, stage, at, slot, at)
+
+    def spread_send(self, stage):
+        self.others(
+            stage, lambda k, me, at: self.spread_copy(stage, k, me, at, False).start()
+        )
+
+    def spread_add(self, stage):
+        self.others(
+            stage, lambda k, me, at: self.spread_copy(stage, k, me, at, True).wait()
+        )
+        size = 4 * self.u if stage == 0 else self.u
+        for k in range(3):
+            me = self.me(k, stage)
+            if stage == 0:
+                total = self.paired[pl.ds((4 * k + me) * size, size)].astype(F32)
+            else:
+                total = self.part[k, pl.ds(me * size, size)].astype(F32)
+            slots = self.slots if stage == 0 else self.slots2
+            for d in range(1, 4):
+                total = total + slots[k, (me + d) % 4].astype(F32)
+            if stage == 0:
+                self.part[k] = total.astype(BF)
+            else:
+                self.own[k] = total.astype(BF)
+
+    def last_copy(self, k, me, at, arriving):
+        slot = at if arriving else me
+        return self.copy(self.own.at[k], self.slots3.at[k, slot], 2, k, 2, at, slot, at)
+
+    def last_send(self):
+        self.others(2, lambda k, me, at: self.last_copy(k, me, at, False).start())
+
+    def last_add(self):
+        self.others(2, lambda k, me, at: self.last_copy(k, me, at, True).wait())
+        for k in range(3):
+            self.slots3[k, self.me(k, 2)] = self.own[k]
+            total = self.slots3[k, 0].astype(F32) + self.slots3[k, 1].astype(F32)
+            total = total + self.slots3[k, 2].astype(F32) + self.slots3[k, 3].astype(F32)
+            self.row[k, pl.ds(self.me(k, 1) * self.u, self.u)] = total.astype(BF)
+
+    def gather_copy(self, stage, k, me, at, arriving):
+        slot = at if arriving else me
+        if stage == 1:
+            mine = self.row.at[k, pl.ds(me * self.u, self.u)]
+            dst = self.row.at[k, pl.ds(slot * self.u, self.u)]
+        else:
+            size = 4 * self.u
+            mine = self.row.at[k]
+            dst = self.fin.at[self.g, pl.ds((4 * k + slot) * size, size)]
+        return self.copy(mine, dst, 4 - stage, k, stage, at, slot, at)
+
+    def gather_send(self, stage):
+        self.others(
+            stage, lambda k, me, at: self.gather_copy(stage, k, me, at, False).start()
+        )
+        if stage == 0:
+            size = 4 * self.u
+            for k in range(3):
+                me = self.me(k, 0)
+                self.fin[self.g, pl.ds((4 * k + me) * size, size)] = self.row[k]
+                self.over(k, me, True).start()
+
+    def gather_wait(self, stage):
+        def step(k, me, at):
+            self.gather_copy(stage, k, me, at, True).wait()
+            if stage == 0:
+                self.over(k, at, True).start()
+
+        self.others(stage, step)
+
+    def over(self, k, at, mine):
+        size = 4 * self.u
+        part = self.fin.at[self.g if mine else 1 - self.g, pl.ds((4 * k + at) * size, size)]
+        return pltpu.make_async_remote_copy(
+            part, part, self.pair.at[0, 4 * k + at], self.pair.at[1, 4 * k + at],
+            device_id={"grp": 1 - self.g}, device_id_type=MESH,
+        )
+
+    def pair_done(self):
+        for k in range(3):
+            for at in range(4):
+                self.over(k, at, True).wait_send()
+                self.over(k, at, False).wait_recv()
+
+
 def main_kernel(
     skip_hbm, grad_hbm, wup_hbm, win_hbm, wout_hbm, sw_hbm, tw_hbm,
-    out, gup, gin, gout,
+    out, fin1, fin2,
     skip, gpad, wup, win, wout, sw, tw,
     a1s, a1r, a2s, a2r, b1s, b1r, b2s, b2r, c1s, c1r, c2s, c2r, d1s, d1r, d2s, d2r,
     pooled_t, coarse_t, pooled_f, coarse_f, gunited, gexp, gexp_t, gtimed, gcoarse,
     qs, ks, vs, probs_s, qt, kt, vt, probs_t, mix, mix_t, attended, timed, gmix, gq, gk, gv, gatt,
     unit_t,
-    load_sem, halo_sem, swap_sem,
+    x1, s1, z1, p1, t1, w1, v1, a1, x2, s2, z2, p2, t2, w2, v2, a2,
+    load_sem, halo_sem, swap_sem, ring_sem1, pair_sem1, ring_sem2, pair_sem2,
 ):
     r, c, g = lax.axis_index("row"), lax.axis_index("col"), lax.axis_index("grp")
     loads = {}
@@ -132,7 +285,14 @@
     for dr, dc in around:
         if dr != 0 and dc != 0:
             pl.semaphore_signal(barrier, 1, device_id=beside(dr, dc), device_id_type=MESH)
-    pl.semaphore_wait(barrier, 2 * (N - 1) + 4)
+    x, y, z = r // 2, (c // 4) * 2 + r % 2, c % 4
+    pl.semaphore_signal(
+        barrier, 1, device_id={"row": x * 2 + (r + 1) % 2, "col": (c + 4) % N}, device_id_type=MESH
+    )
+    pl.semaphore_signal(barrier, 1, device_id={"grp": 1 - g}, device_id_type=MESH)
+    pl.semaphore_wait(barrier, 2 * (N - 1) + 6)
+    first = Sum((x, y, z), g, x1, s1, z1, p1, t1, w1, v1, a1, fin1, ring_sem1, pair_sem1)
+    second = Sum((x, y, z), g, x2, s2, z2, p2, t2, w2, v2, a2, fin2, ring_sem2, pair_sem2)
 
     def send(stage, src, dst, axis, me):
         dst[me] = src[me]
@@ -181,6 +341,10 @@
     loads["grad"].wait()
     for k in range(8):
         halo(k).start()
+    x1[0, 140:144] = jnp.zeros((4,) + x1.shape[2:], BF)
+    x1[1, 120:144] = jnp.zeros((24,) + x1.shape[2:], BF)
+    for half in range(2):
+        x2[half, 40:48] = jnp.zeros((8,) + x2.shape[2:], BF)
 
     loads["skip"].wait()
     means = []
@@ -276,7 +440,9 @@
     send(4, c1s, c1r, "row", r)
 
     wide_nt(attended, [(mix, tw, 3)], timed)
-    gout[...] = dot_tn(gexp_t[...], timed[...])
+    for k in range(4):
+        part = dot_tn(gexp_t[...], timed[:, k * chan:(k + 1) * chan])
+        x1[1, 40 + 20 * k:60 + 20 * k] = part.astype(BF).reshape(20, 16, chan)
     expanded = dot_nt(timed[...], wout[...])
     for p in range(2):
         rows = jnp.concatenate(
@@ -296,22 +462,41 @@
     def tap_step(tap, carry):
         dy, dx = tap // 3, tap % 3
         rows = gpad[pl.ds(2 - dy, 8), pl.ds(2 - dx, 4)].reshape(2048, chan)
-        gup[tap] = dot(unit_t[...], rows)
+        owner = tap // 7
+        x1[owner, pl.ds(20 * (tap - 7 * owner), 20)] = (
+            dot(unit_t[...], rows).astype(BF).reshape(20, 16, chan)
+        )
         return carry
 
     lax.fori_loop(0, 9, tap_step, 0)
+    first.pair_send()
     arrive(5, c2s, c2r, "col", c)
     gatt[...] = c2r[...].reshape(gatt.shape)
 
     gmix[...] = dot(gatt[...], sw[3]).astype(BF)
+    first.pair_add()
+    first.spread_send(0)
     attend_back(qs, ks, vs, probs_s, gmix, gq, gk, gv)
+    first.spread_add(0)
+    first.spread_send(1)
     wide_nt(gatt, [(gq, sw, 0), (gk, sw, 1), (gv, sw, 2)], gcoarse)
     d1s[...] = dot_nt(gcoarse[...], win[...]).astype(BF).reshape(d1s.shape)
     send(6, d1s, d1r, "col", c)
-    gin[...] = dot_tn(pooled_f[...], gcoarse[...])
+    first.spread_add(1)
+    first.last_send()
+    for k in range(4):
+        part = dot_tn(pooled_f[...], gcoarse[:, k * chan:(k + 1) * chan])
+        x2[k // 2, 20 * (k % 2):20 * (k % 2) + 20] = part.astype(BF).reshape(20, 16, chan)
+    second.pair_send()
     arrive(6, d1s, d1r, "col", c)
     turn(d1r, d2s, True)
     send(7, d2s, d2r, "row", r)
+    first.last_add()
+    first.gather_send(1)
+    second.pair_add()
+    second.spread_send(0)
+    first.gather_wait(1)
+    first.gather_send(0)
     arrive(7, d2s, d2r, "row", r)
     spread = d2r[...].reshape(128, chan).astype(F32) * (1.0 / (POOL * POOL))
     for p in range(2):
@@ -324,6 +509,18 @@
             return carry
 
         lax.fori_loop(p * POOL, p * POOL + POOL, finish, 0)
+    second.spread_add(0)
+    second.spread_send(1)
+    first.gather_wait(0)
+    second.spread_add(1)
+    second.last_send()
+    second.last_add()
+    second.gather_send(1)
+    second.gather_wait(1)
+    second.gather_send(0)
+    second.gather_wait(0)
+    first.pair_done()
+    second.pair_done()
 
 
 def shards(skip, w_up, w_in, w_out, spatial_w, temporal_w, grad_out):
@@ -341,6 +538,15 @@
     swaps = []
     for width in (chan, att, wide, chan):
         swaps += [vm((N, 16, width))] * 4
+
+    def sums(u):
+        block = (16, chan)
+        return [
+            vm((2, 48 * u) + block), vm((48 * u,) + block), vm((3, 4, 4 * u) + block),
+            vm((3, 4 * u) + block), vm((3, 4, u) + block), vm((3, u) + block),
+            vm((3, 4, u) + block), vm((3, 4 * u) + block),
+        ]
+
     scratch = [
         vm(skip_t.shape), vm((tile_h + 2, tile_w + 2, frames, chan)), vm(w_up.shape),
         vm(w_in.shape), vm(w_out_t.shape), vm(spatial_w.shape), vm(temporal_w.shape),
@@ -353,27 +559,34 @@
         vm((tok, att)), vm((tok, att)), vm((tok, wide)), vm((tok, wide)),
         vm((tok, att)), vm((tok, att)), vm((tok, att)), vm((tok, att)), vm((tok, wide)),
         vm((chan, frames * tile_h * tile_w)),
+        *sums(3), *sums(1),
         pltpu.SemaphoreType.DMA((7,)), pltpu.SemaphoreType.DMA((2, 8)),
         pltpu.SemaphoreType.DMA((8, 2, N)),
+        *[pltpu.SemaphoreType.DMA((5, 2, 3, 4)), pltpu.SemaphoreType.DMA((2, 13))] * 2,
     ]
-    grad_skip, grad_w_up, grad_w_in, grad_w_out = pl.pallas_call(
+    grad_skip, sum1, sum2 = pl.pallas_call(
         main_kernel,
         out_shape=(
             jax.ShapeDtypeStruct(skip_t.shape, BF),
-            jax.ShapeDtypeStruct(w_up.shape, F32),
-            jax.ShapeDtypeStruct(w_in.shape, F32),
-            jax.ShapeDtypeStruct(w_out_t.shape, F32),
+            jax.ShapeDtypeStruct((2, 144, 16, chan), BF),
+            jax.ShapeDtypeStruct((2, 48, 16, chan), BF),
         ),
         in_specs=[pl.BlockSpec(memory_space=pl.ANY)] * 7,
-        out_specs=[pl.BlockSpec(memory_space=pltpu.VMEM)] * 4,
+        out_specs=[pl.BlockSpec(memory_space=pltpu.VMEM)] * 3,
         scratch_shapes=scratch,
         compiler_params=pltpu.CompilerParams(
             collective_id=0, has_side_effects=True, vmem_limit_bytes=60 * 1024 * 1024
         ),
         name="backward",
     )(skip_t, grad_t, w_up, w_in, w_out_t, spatial_w, temporal_w)
-    grads = lax.psum((grad_w_up, grad_w_in, grad_w_out), ("row", "col", "grp"))
-    return (jnp.transpose(grad_skip, (2, 0, 1, 3)), grads[0], grads[1], grads[2].T)
+    up = jnp.concatenate([sum1[0, :140], sum1[1, :40]], axis=0).reshape(w_up.shape).astype(F32)
+
+    def wide_of(blocks):
+        return jnp.swapaxes(blocks.reshape(4, chan, chan), 0, 1).reshape(chan, wide).astype(F32)
+
+    grad_w_out = wide_of(sum1[1, 40:120]).T
+    grad_w_in = wide_of(jnp.concatenate([sum2[0, :40], sum2[1, :40]], axis=0))
+    return (jnp.transpose(grad_skip, (2, 0, 1, 3)), up, grad_w_in, grad_w_out)
 
 
 def solution(mesh):

time: 283 us -> 159 us (0.56)
  waiting for transfers between devices: 161 us -> 0 us
  Pallas kernels: 90.9 us -> 133 us
  between operations: 14 us -> 0.7 us
  local copies, waits for them, and re-layouts: 16.3 us -> 22.1 us
  other arithmetic: 0 us -> 3.26 us
    psum x1 -> x0, waiting for transfers between devices: 161 us -> none  [shards(): grads = lax.psum((grad_w_up, grad_w_in, grad_w_out), ('row', 'col', 'grp'))]
    pallas_call x1, Pallas kernels: 90.9 us -> 133 us  [shards(): pl.pallas_call(main_kernel, out_shape=(jax.ShapeDtypeStruct(skip_t.shape,...]
    convert_element_type x0 -> x2, local copies, waits for them, and re-layouts: none -> 5.72 us  [wide_of(): jnp.swapaxes(blocks.reshape(4, chan, chan), 0, 1).reshape(chan, wide)]
    unnamed x10 -> x7, local copies, waits for them, and re-layouts: 11.7 us -> 8.68 us
  transfers between devices with their start and end apart: 1 -> 0, of which waited for: 1 -> 0; matrix products, arithmetic and copies ran while one was open for 1% -> 0% of each run, Pallas kernels for 0% -> 0%
where the time goes in v2:
time: 159 us
  Pallas kernels  133 us (84%)
  local copies, waits for them, and re-layouts  22.1 us (14%)
  other arithmetic  3.26 us (2%)
    pallas_call x1, Pallas kernels, shards(): pl.pallas_call(main_kernel, out_shape=(jax.ShapeDtypeStruct(skip_t.shape,...  133 us
    unnamed x7, local copies, waits for them, and re-layouts  8.68 us
    convert_element_type x2, local copies, waits for them, and re-layouts, wide_of(): jnp.swapaxes(blocks.reshape(4, chan, chan), 0, 1).reshape(chan, wide)  5.72 us
    transpose x2, local copies, waits for them, and re-layouts, shards(): grad_w_out = wide_of(sum1[1, 40:120]).T  3.59 us

profile of v2, /device:TPU:1, one launch (start us, length us, event | category | flops | bytes accessed | tf_op | source)
XLA Modules:
  0.0 158.7 jit_solution(15141732004120739077)
XLA Ops:
  0.6 0.0 copy-start
  0.6 3.2 %copy.19 = bf16[64,8,4,320]{3,0,2,1:T(8,128)(2,1)} copy(bf16[64,8,4,320]{3,2,1,0:T(4,128)(2,1)} %param.7) | data formatting | bytes 2621440 | tf_op args[0]
  3.8 0.0 copy-done
  3.8 1.7 %copy.18 = bf16[64,8,4,320]{3,0,2,1:T(8,128)(2,1)} copy(bf16[64,8,4,320]{3,2,1,0:T(4,128)(2,1)S(1)} %copy-done) | data formatting | bytes 2621440 | tf_op args[6]
  5.5 132.7 %backward.1 = (bf16[8,4,64,320]{3,2,1,0:T(8,128)(2,1)}, bf16[2,144,16,320]{3,2,1,0:T(8,128)(2,1)}, bf16[2,48,16,320]{3,2,1,0:T(8,128)(2,1)}) custom-call(bf16[8,4,64,320]{3,2,1,0:T(8,128)(2,1)} %bitcast.32, bf16[8,4,64,320]{3,2,1,0:T(8,128)(2,1)} %bitcast.33, bf16[9,320,320]{2,1,0:T(8,128)(2,1)} %wup_hbm.1, bf16[320,1280]{1,0:T(8,128)(2,1)} %win_hbm.1, ...), custom_call_target="tpu_custom_call" | custom-call | tf_op jit(solution)/shard_map/backward/pallas_call | solution.py:567
  138.2 3.8 %copy.15 = bf16[64,8,4,320]{3,2,1,0:T(4,128)(2,1)} copy(bf16[64,8,4,320]{3,0,2,1:T(8,128)(2,1)} %bitcast.37) | data formatting | bytes 2621440
  142.0 1.3 slice.19
  143.3 0.1 convert_bitcast_fusion
  143.4 1.3 copy.14
  144.7 0.0 copy-start.1
  144.7 2.3 %reshape.24 = f32[320,1280]{1,0:T(8,128)} reshape(f32[320,4,320]{2,1,0:T(4,128)S(1)} %copy.14) | data formatting | bytes 3276800 | tf_op jit(solution)/shard_map/transpose | solution.py:587
  147.1 0.0 copy-done.1
  147.1 1.2 slice_bitcast_fusion.2
  148.2 1.6 %slice_bitcast_fusion = bf16[140,16,320]{2,1,0:T(8,128)(2,1)S(1)} fusion(bf16[2,144,16,320]{3,2,1,0:T(8,128)(2,1)} %get-tuple-element.8), kind=kLoop, calls=%fused_computation.4 | loop fusion | bytes 2867200 | tf_op jit(solution)/shard_map/squeeze | solution.py:582
  149.9 0.2 pad_maximum_fusion.1
  150.1 0.4 pad_maximum_fusion
  150.5 0.1 convert_bitcast_fusion.1
  150.6 2.5 %copy.13 = f32[320,4,320]{2,1,0:T(4,128)} copy(f32[320,4,320]{2,0,1:T(8,128)S(1)} %convert_bitcast_fusion.1) | data formatting | bytes 3276800 | tf_op jit(solution)/shard_map/convert_element_type | solution.py:585
  153.1 3.2 %reshape.23 = f32[320,1280]{1,0:T(8,128)} reshape(f32[320,4,320]{2,1,0:T(4,128)} %copy.13) | data formatting | bytes 3276800 | tf_op jit(solution)/shard_map/convert_element_type | solution.py:585
  156.3 2.4 %bitcast_convert_fusion = f32[9,320,320]{2,1,0:T(8,128)} fusion(bf16[9,320,320]{2,1,0:T(8,128)(2,1)S(1)} %bitcast.31), kind=kLoop, calls=%fused_computation.1 | loop fusion | flops 921600 | bytes 5529600 | tf_op jit(solution)/shard_map/convert_element_type | solution.py:582
Async XLA Ops:
  0.6 3.2 %copy-start = (bf16[64,8,4,320]{3,2,1,0:T(4,128)(2,1)S(1)}, bf16[64,8,4,320]{3,2,1,0:T(4,128)(2,1)}, u32[]{:S(2)}) copy-start(bf16[64,8,4,320]{3,2,1,0:T(4,128)(2,1)} %param.13) | copy-start | bytes 3932164
  144.7 2.3 %copy-start.1 = (bf16[2,48,16,320]{3,2,1,0:T(8,128)(2,1)S(1)}, bf16[2,48,16,320]{3,2,1,0:T(8,128)(2,1)}, u32[]{:S(2)}) copy-start(bf16[2,48,16,320]{3,2,1,0:T(8,128)(2,1)} %get-tuple-element.9) | copy-start | bytes 2949124

commit v3 on v2

--- a/solution.py
+++ b/solution.py
@@ -11,6 +11,8 @@
 F32 = jnp.float32
 BF = jnp.bfloat16
 MESH = pl.DeviceIdType.MESH
+SIZES1 = (7, 7, 7)
+SIZES2 = (3, 2, 2)
 
 
 def dot(a, b):
@@ -96,13 +98,43 @@
     lax.fori_loop(0, out.shape[1] // 256, step, 0)
 
 
+def put(units, group, product):
+    for n in range(product.shape[1] // 128):
+        part = product[:, 128 * n:128 * n + 128].astype(BF).reshape(-1, 16, 128)
+        size = part.shape[0]
+        units[pl.ds((group + n) * size, size)] = part
+
+
+def wide_tn(left, right, units, group):
+    def step(at, carry):
+        cols = pl.ds(pl.multiple_of(at * 256, 256), 256)
+        put(units, group + 2 * at, dot_tn(left[...], right[:, cols]))
+        return carry
+
+    lax.fori_loop(0, right.shape[1] // 256, step, 0)
+
+
 class Sum:
-    def __init__(self, place, g, blocks, paired, slots, part, slots2, own, slots3, row, fin, ring, pair):
-        self.place, self.g = place, g
+    def __init__(self, place, g, sizes, blocks, paired, slots, part, slots2, own, slots3, row, fin,
+                 ring, pair):
+        self.place, self.g, self.sizes = place, g, sizes
         self.blocks, self.paired, self.slots, self.part = blocks, paired, slots, part
         self.slots2, self.own, self.slots3, self.row, self.fin = slots2, own, slots3, row, fin
         self.ring, self.pair = ring, pair
-        self.u = blocks.shape[1] // 48
+        self.offs = [sum(sizes[:k]) for k in range(3)]
+        self.total = 16 * sum(sizes)
+
+    def big(self, k, at, base=0):
+        return pl.ds(base + 16 * self.offs[k] + at * (4 * self.sizes[k]), 4 * self.sizes[k])
+
+    def small(self, k, at):
+        return pl.ds(4 * self.offs[k] + at * self.sizes[k], self.sizes[k])
+
+    def line(self, k):
+        return pl.ds(4 * self.offs[k], 4 * self.sizes[k])
+
+    def mine(self, k):
+        return pl.ds(self.offs[k], self.sizes[k])
 
     def me(self, k, stage):
         return self.place[(k + stage) % 3]
@@ -132,37 +164,41 @@
 
             lax.fori_loop(1, 4, one, 0)
 
-    def pair_copy(self):
+    def quarters(self, step):
+        for k in range(3):
+            def one(at, carry):
+                step(k, at)
+                return carry
+
+            lax.fori_loop(0, 4, one, 0)
+
+    def pair_copy(self, k, at):
         return pltpu.make_async_remote_copy(
-            self.blocks.at[1 - self.g], self.paired, self.pair.at[0, 12], self.pair.at[1, 12],
+            self.blocks.at[self.big(k, at, (1 - self.g) * self.total)],
+            self.paired.at[self.big(k, at)],
+            self.pair.at[0, 0, 4 * k + at], self.pair.at[0, 1, 4 * k + at],
             device_id={"grp": 1 - self.g}, device_id_type=MESH,
         )
 
     def pair_send(self):
-        self.pair_copy().start()
+        self.quarters(lambda k, at: self.pair_copy(k, at).start())
 
     def pair_add(self):
-        self.pair_copy().wait()
-        size = 4 * self.u
-
-        def step(at, carry):
-            some = pl.ds(at * size, size)
-            total = self.blocks[self.g, some].astype(F32) + self.paired[some].astype(F32)
-            self.paired[some] = total.astype(BF)
-            return carry
-
-        lax.fori_loop(0, 12, step, 0)
+        def step(k, at):
+            self.pair_copy(k, at).wait()
+            some = self.big(k, at)
+            total = self.blocks[self.big(k, at, self.g * self.total)].astype(F32)
+            self.paired[some] = (total + self.paired[some].astype(F32)).astype(BF)
+
+        self.quarters(step)
 
     def spread_copy(self, stage, k, me, at, arriving):
+        slot = at if arriving else me
         if stage == 0:
-            size = 4 * self.u
-            src = self.paired.at[pl.ds((4 * k + at) * size, size)]
-            slots = self.slots
+            src, dst = self.paired.at[self.big(k, at)], self.slots.at[self.big(k, slot)]
         else:
-            src = self.part.at[k, pl.ds(at * self.u, self.u)]
-            slots = self.slots2
-        slot = at if arriving else me
-        return self.copy(src, slots.at[k, slot], stage, k, stage, at, slot, at)
+            src, dst = self.part.at[self.small(k, at)], self.slots2.at[self.small(k, slot)]
+        return self.copy(src, dst, stage, k, stage, at, slot, at)
 
     def spread_send(self, stage):
         self.others(
@@ -170,27 +206,29 @@
         )
 
     def spread_add(self, stage):
-        self.others(
-            stage, lambda k, me, at: self.spread_copy(stage, k, me, at, True).wait()
-        )
-        size = 4 * self.u if stage == 0 else self.u
         for k in range(3):
             me = self.me(k, stage)
+
+            def one(d, carry):
+                self.spread_copy(stage, k, me, (me + d) % 4, True).wait()
+                return carry
+
+            lax.fori_loop(1, 4, one, 0)
             if stage == 0:
-                total = self.paired[pl.ds((4 * k + me) * size, size)].astype(F32)
+                total = self.paired[self.big(k, me)].astype(F32)
+                for d in range(1, 4):
+                    total = total + self.slots[self.big(k, (me + d) % 4)].astype(F32)
+                self.part[self.line(k)] = total.astype(BF)
             else:
-                total = self.part[k, pl.ds(me * size, size)].astype(F32)
-            slots = self.slots if stage == 0 else self.slots2
-            for d in range(1, 4):
-                total = total + slots[k, (me + d) % 4].astype(F32)
-            if stage == 0:
-                self.part[k] = total.astype(BF)
-            else:
-                self.own[k] = total.astype(BF)
+                total = self.part[self.small(k, me)].astype(F32)
+                for d in range(1, 4):
+                    total = total + self.slots2[self.small(k, (me + d) % 4)].astype(F32)
+                self.own[self.mine(k)] = total.astype(BF)
 
     def last_copy(self, k, me, at, arriving):
         slot = at if arriving else me
-        return self.copy(self.own.at[k], self.slots3.at[k, slot], 2, k, 2, at, slot, at)
+        dst = self.slots3.at[self.small(k, slot)]
+        return self.copy(self.own.at[self.mine(k)], dst, 2, k, 2, at, slot, at)
 
     def last_send(self):
         self.others(2, lambda k, me, at: self.last_copy(k, me, at, False).start())
@@ -198,31 +236,29 @@
     def last_add(self):
         self.others(2, lambda k, me, at: self.last_copy(k, me, at, True).wait())
         for k in range(3):
-            self.slots3[k, self.me(k, 2)] = self.own[k]
-            total = self.slots3[k, 0].astype(F32) + self.slots3[k, 1].astype(F32)
-            total = total + self.slots3[k, 2].astype(F32) + self.slots3[k, 3].astype(F32)
-            self.row[k, pl.ds(self.me(k, 1) * self.u, self.u)] = total.astype(BF)
+            self.slots3[self.small(k, self.me(k, 2))] = self.own[self.mine(k)]
+            total = self.slots3[self.small(k, 0)].astype(F32)
+            for at in range(1, 4):
+                total = total + self.slots3[self.small(k, at)].astype(F32)
+            self.row[self.small(k, self.me(k, 1))] = total.astype(BF)
 
     def gather_copy(self, stage, k, me, at, arriving):
         slot = at if arriving else me
         if stage == 1:
-            mine = self.row.at[k, pl.ds(me * self.u, self.u)]
-            dst = self.row.at[k, pl.ds(slot * self.u, self.u)]
+            src, dst = self.row.at[self.small(k, me)], self.row.at[self.small(k, slot)]
         else:
-            size = 4 * self.u
-            mine = self.row.at[k]
-            dst = self.fin.at[self.g, pl.ds((4 * k + slot) * size, size)]
-        return self.copy(mine, dst, 4 - stage, k, stage, at, slot, at)
+            src = self.row.at[self.line(k)]
+            dst = self.fin.at[self.big(k, slot, self.g * self.total)]
+        return self.copy(src, dst, 4 - stage, k, stage, at, slot, at)
 
     def gather_send(self, stage):
         self.others(
             stage, lambda k, me, at: self.gather_copy(stage, k, me, at, False).start()
         )
         if stage == 0:
-            size = 4 * self.u
             for k in range(3):
                 me = self.me(k, 0)
-                self.fin[self.g, pl.ds((4 * k + me) * size, size)] = self.row[k]
+                self.fin[self.big(k, me, self.g * self.total)] = self.row[self.line(k)]
                 self.over(k, me, True).start()
 
     def gather_wait(self, stage):
@@ -234,43 +270,68 @@
         self.others(stage, step)
 
     def over(self, k, at, mine):
-        size = 4 * self.u
-        part = self.fin.at[self.g if mine else 1 - self.g, pl.ds((4 * k + at) * size, size)]
+        half = self.g if mine else 1 - self.g
+        part = self.fin.at[self.big(k, at, half * self.total)]
         return pltpu.make_async_remote_copy(
-            part, part, self.pair.at[0, 4 * k + at], self.pair.at[1, 4 * k + at],
+            part, part, self.pair.at[1, 0, 4 * k + at], self.pair.at[1, 1, 4 * k + at],
             device_id={"grp": 1 - self.g}, device_id_type=MESH,
         )
 
     def pair_done(self):
-        for k in range(3):
-            for at in range(4):
-                self.over(k, at, True).wait_send()
-                self.over(k, at, False).wait_recv()
+        def step(k, at):
+            self.over(k, at, True).wait_send()
+            self.over(k, at, False).wait_recv()
+
+        self.quarters(step)
+
+
+class Loads:
+    def __init__(self, copies):
+        self.copies = copies
+
+    def start(self):
+        for copy in self.copies:
+            copy.start()
+
+    def wait(self):
+        for copy in self.copies:
+            copy.wait()
+
+
+def cut_rows(ref, count):
+    size = ref.shape[1] // count
+    return [pl.ds(size * n, size) for n in range(count)]
 
 
 def main_kernel(
     skip_hbm, grad_hbm, wup_hbm, win_hbm, wout_hbm, sw_hbm, tw_hbm,
-    out, fin1, fin2,
+    out, up_out, wide_out,
     skip, gpad, wup, win, wout, sw, tw,
     a1s, a1r, a2s, a2r, b1s, b1r, b2s, b2r, c1s, c1r, c2s, c2r, d1s, d1r, d2s, d2r,
     pooled_t, coarse_t, pooled_f, coarse_f, gunited, gexp, gexp_t, gtimed, gcoarse,
     qs, ks, vs, probs_s, qt, kt, vt, probs_t, mix, mix_t, attended, timed, gmix, gq, gk, gv, gatt,
     unit_t,
-    x1, s1, z1, p1, t1, w1, v1, a1, x2, s2, z2, p2, t2, w2, v2, a2,
+    x1, s1, z1, p1, t1, w1, v1, a1, fin1, x2, s2, z2, p2, t2, w2, v2, a2, fin2,
     load_sem, halo_sem, swap_sem, ring_sem1, pair_sem1, ring_sem2, pair_sem2,
 ):
     r, c, g = lax.axis_index("row"), lax.axis_index("col"), lax.axis_index("grp")
     loads = {}
-    for at, (name, src, dst) in enumerate((
-        ("grad", grad_hbm, gpad.at[1:9, 1:5]),
-        ("skip", skip_hbm, skip),
-        ("win", win_hbm, win),
-        ("wup", wup_hbm, wup),
-        ("wout", wout_hbm, wout),
-        ("sw", sw_hbm, sw),
-        ("tw", tw_hbm, tw),
-    )):
-        loads[name] = pltpu.make_async_copy(src, dst, load_sem.at[at])
+    load_at = 0
+    for name, pieces in (
+        ("skip", [(skip_hbm.at[i], skip.at[i]) for i in range(8)]),
+        ("grad", [(grad_hbm.at[i], gpad.at[1 + i, 1:5]) for i in range(8)]),
+        ("win", [(win_hbm, win)]),
+        ("sw", [(sw_hbm.at[m, h], sw.at[m, h]) for m in range(4) for h in cut_rows(sw, 4)]),
+        ("wout", [(wout_hbm, wout)]),
+        ("tw", [(tw_hbm.at[m, h], tw.at[m, h]) for m in range(4) for h in cut_rows(tw, 4)]),
+        ("wup", [(wup_hbm.at[m], wup.at[m]) for m in range(9)]),
+    ):
+        loads[name] = Loads(
+            [pltpu.make_async_copy(src, dst, load_sem.at[load_at + n])
+             for n, (src, dst) in enumerate(pieces)]
+        )
+        load_at += len(pieces)
+    for name in ("skip", "grad", "win", "sw"):
         loads[name].start()
 
     around = [(dr, dc) for dr in (-1, 0, 1) for dc in (-1, 0, 1) if (dr, dc) != (0, 0)]
@@ -291,8 +352,12 @@
     )
     pl.semaphore_signal(barrier, 1, device_id={"grp": 1 - g}, device_id_type=MESH)
     pl.semaphore_wait(barrier, 2 * (N - 1) + 6)
-    first = Sum((x, y, z), g, x1, s1, z1, p1, t1, w1, v1, a1, fin1, ring_sem1, pair_sem1)
-    second = Sum((x, y, z), g, x2, s2, z2, p2, t2, w2, v2, a2, fin2, ring_sem2, pair_sem2)
+    first = Sum(
+        (x, y, z), g, SIZES1, x1, s1, z1, p1, t1, w1, v1, a1, fin1, ring_sem1, pair_sem1
+    )
+    second = Sum(
+        (x, y, z), g, SIZES2, x2, s2, z2, p2, t2, w2, v2, a2, fin2, ring_sem2, pair_sem2
+    )
 
     def send(stage, src, dst, axis, me):
         dst[me] = src[me]
@@ -338,14 +403,6 @@
             device_id=beside(dr, dc), device_id_type=MESH,
         )
 
-    loads["grad"].wait()
-    for k in range(8):
-        halo(k).start()
-    x1[0, 140:144] = jnp.zeros((4,) + x1.shape[2:], BF)
-    x1[1, 120:144] = jnp.zeros((24,) + x1.shape[2:], BF)
-    for half in range(2):
-        x2[half, 40:48] = jnp.zeros((8,) + x2.shape[2:], BF)
-
     loads["skip"].wait()
     means = []
     for p in range(2):
@@ -359,29 +416,15 @@
         a1s[f] = rows.astype(BF)
     pooled_t[...] = a1s[...].reshape(128, -1)
     send(0, a1s, a1r, "row", r)
-
+    loads["grad"].wait()
+    for k in range(8):
+        halo(k).start()
+    for name in ("wout", "tw", "wup"):
+        loads[name].start()
+    x1[660:] = jnp.zeros((12,) + x1.shape[1:], BF)
+    x2[200:] = jnp.zeros((24,) + x2.shape[1:], BF)
     loads["win"].wait()
     coarse_t[...] = dot(pooled_t[...], win[...]).astype(BF)
-    loads["wup"].wait()
-    for k in range(8):
-        halo(k).wait()
-
-    @pl.when(r == 0)
-    def _():
-        gpad[0] = jnp.zeros(gpad.shape[1:], BF)
-
-    @pl.when(r == N - 1)
-    def _():
-        gpad[9] = jnp.zeros(gpad.shape[1:], BF)
-
-    @pl.when(c == 0)
-    def _():
-        gpad[:, 0] = jnp.zeros((10,) + gpad.shape[2:], BF)
-
-    @pl.when(c == N - 1)
-    def _():
-        gpad[:, 5] = jnp.zeros((10,) + gpad.shape[2:], BF)
-
     chan = gpad.shape[3]
     gexp[...] = jnp.zeros_like(gexp)
 
@@ -399,11 +442,9 @@
 
         lax.fori_loop(first, last, step, 0)
 
-    back_rows(0, 3)
     arrive(0, a1s, a1r, "row", r)
     turn(a1r, a2s, False)
     send(1, a2s, a2r, "col", c)
-    back_rows(3, 6)
     arrive(1, a2s, a2r, "col", c)
     pooled_f[...] = a2r[...].reshape(128, chan)
 
@@ -414,12 +455,33 @@
     attend(qs, ks, vs, probs_s, mix, None)
     b1s[...] = mix[...].reshape(b1s.shape)
     send(2, b1s, b1r, "col", c)
-    back_rows(6, 8)
+    loads["wup"].wait()
+    for k in range(8):
+        halo(k).wait()
+
+    @pl.when(r == 0)
+    def _():
+        gpad[0] = jnp.zeros(gpad.shape[1:], BF)
+
+    @pl.when(r == N - 1)
+    def _():
+        gpad[9] = jnp.zeros(gpad.shape[1:], BF)
+
+    @pl.when(c == 0)
+    def _():
+        gpad[:, 0] = jnp.zeros((10,) + gpad.shape[2:], BF)
+
+    @pl.when(c == N - 1)
+    def _():
+        gpad[:, 5] = jnp.zeros((10,) + gpad.shape[2:], BF)
+
+    back_rows(0, 4)
     arrive(2, b1s, b1r, "col", c)
     turn(b1r, b2s, True)
     send(3, b2s, b2r, "row", r)
     loads["wout"].wait()
     loads["tw"].wait()
+    back_rows(4, 8)
     for f in range(N):
         rows = jnp.concatenate([gexp[0, 8 * f:8 * f + 8], gexp[1, 8 * f:8 * f + 8]], axis=0)
         gexp_t[16 * f:16 * f + 16] = rows.astype(BF)
@@ -440,9 +502,7 @@
     send(4, c1s, c1r, "row", r)
 
     wide_nt(attended, [(mix, tw, 3)], timed)
-    for k in range(4):
-        part = dot_tn(gexp_t[...], timed[:, k * chan:(k + 1) * chan])
-        x1[1, 40 + 20 * k:60 + 20 * k] = part.astype(BF).reshape(20, 16, chan)
+    wide_tn(gexp_t, timed, x1, 23)
     expanded = dot_nt(timed[...], wout[...])
     for p in range(2):
         rows = jnp.concatenate(
@@ -459,16 +519,20 @@
     turn(c1r, c2s, False)
     send(5, c2s, c2r, "col", c)
 
+    def tap_rows(tap, cols):
+        dy, dx = tap // 3, tap % 3
+        return gpad[pl.ds(2 - dy, 8), pl.ds(2 - dx, 4), :, cols].reshape(2048, -1)
+
     def tap_step(tap, carry):
-        dy, dx = tap // 3, tap % 3
-        rows = gpad[pl.ds(2 - dy, 8), pl.ds(2 - dx, 4)].reshape(2048, chan)
-        owner = tap // 7
-        x1[owner, pl.ds(20 * (tap - 7 * owner), 20)] = (
-            dot(unit_t[...], rows).astype(BF).reshape(20, 16, chan)
-        )
+        put(x1, 2 * tap, dot(unit_t[...], tap_rows(tap, slice(0, 256))))
         return carry
 
     lax.fori_loop(0, 9, tap_step, 0)
+    for taps, at in (((0, 1, 2, 3), 18), ((4, 5, 6, 7), 20)):
+        rows = jnp.concatenate([tap_rows(tap, slice(256, chan)) for tap in taps], axis=1)
+        put(x1, at, dot(unit_t[...], rows))
+    rows = jnp.concatenate([tap_rows(8, slice(256, chan))] * 2, axis=1)
+    put(x1, 22, dot(unit_t[...], rows))
     first.pair_send()
     arrive(5, c2s, c2r, "col", c)
     gatt[...] = c2r[...].reshape(gatt.shape)
@@ -484,9 +548,7 @@
     send(6, d1s, d1r, "col", c)
     first.spread_add(1)
     first.last_send()
-    for k in range(4):
-        part = dot_tn(pooled_f[...], gcoarse[:, k * chan:(k + 1) * chan])
-        x2[k // 2, 20 * (k % 2):20 * (k % 2) + 20] = part.astype(BF).reshape(20, 16, chan)
+    wide_tn(pooled_f, gcoarse, x2, 0)
     second.pair_send()
     arrive(6, d1s, d1r, "col", c)
     turn(d1r, d2s, True)
@@ -520,7 +582,33 @@
     second.gather_send(0)
     second.gather_wait(0)
     first.pair_done()
+
+    def group_of(fin, at):
+        return fin[pl.ds(20 * at, 20)].reshape(chan, 128)
+
+    def whole(at, carry):
+        up_out[at // 2, :, lanes(at % 2)] = group_of(fin1, at)
+        return carry
+
+    lax.fori_loop(0, 18, whole, 0)
+    for at in range(5):
+        rest = group_of(fin1, 18 + at)
+        up_out[2 * at, :, 256:chan] = rest[:, :chan - 256]
+        if at < 4:
+            up_out[2 * at + 1, :, 256:chan] = rest[:, chan - 256:]
+
+    def wide_group(at, carry):
+        wide_out[0, :, lanes(at)] = group_of(fin1, 23 + at)
+        return carry
+
+    lax.fori_loop(0, 10, wide_group, 0)
     second.pair_done()
+
+    def wide_group2(at, carry):
+        wide_out[1, :, lanes(at)] = group_of(fin2, at)
+        return carry
+
+    lax.fori_loop(0, 10, wide_group2, 0)
 
 
 def shards(skip, w_up, w_in, w_out, spatial_w, temporal_w, grad_out):
@@ -539,13 +627,9 @@
     for width in (chan, att, wide, chan):
         swaps += [vm((N, 16, width))] * 4
 
-    def sums(u):
-        block = (16, chan)
-        return [
-            vm((2, 48 * u) + block), vm((48 * u,) + block), vm((3, 4, 4 * u) + block),
-            vm((3, 4 * u) + block), vm((3, 4, u) + block), vm((3, u) + block),
-            vm((3, 4, u) + block), vm((3, 4 * u) + block),
-        ]
+    def sums(sizes):
+        u = sum(sizes)
+        return [vm((n * u, 16, 128)) for n in (32, 16, 16, 4, 4, 1, 4, 4, 32)]
 
     scratch = [
         vm(skip_t.shape), vm((tile_h + 2, tile_w + 2, frames, chan)), vm(w_up.shape),
@@ -559,17 +643,17 @@
         vm((tok, att)), vm((tok, att)), vm((tok, wide)), vm((tok, wide)),
         vm((tok, att)), vm((tok, att)), vm((tok, att)), vm((tok, att)), vm((tok, wide)),
         vm((chan, frames * tile_h * tile_w)),
-        *sums(3), *sums(1),
-        pltpu.SemaphoreType.DMA((7,)), pltpu.SemaphoreType.DMA((2, 8)),
+        *sums(SIZES1), *sums(SIZES2),
+        pltpu.SemaphoreType.DMA((59,)), pltpu.SemaphoreType.DMA((2, 8)),
         pltpu.SemaphoreType.DMA((8, 2, N)),
-        *[pltpu.SemaphoreType.DMA((5, 2, 3, 4)), pltpu.SemaphoreType.DMA((2, 13))] * 2,
+        *[pltpu.SemaphoreType.DMA((5, 2, 3, 4)), pltpu.SemaphoreType.DMA((2, 2, 12))] * 2,
     ]
-    grad_skip, sum1, sum2 = pl.pallas_call(
+    grad_skip, up, wide_grads = pl.pallas_call(
         main_kernel,
         out_shape=(
             jax.ShapeDtypeStruct(skip_t.shape, BF),
-            jax.ShapeDtypeStruct((2, 144, 16, chan), BF),
-            jax.ShapeDtypeStruct((2, 48, 16, chan), BF),
+            jax.ShapeDtypeStruct(w_up.shape, BF),
+            jax.ShapeDtypeStruct((2,) + w_in.shape, BF),
         ),
         in_specs=[pl.BlockSpec(memory_space=pl.ANY)] * 7,
         out_specs=[pl.BlockSpec(memory_space=pltpu.VMEM)] * 3,
@@ -579,14 +663,8 @@
         ),
         name="backward",
     )(skip_t, grad_t, w_up, w_in, w_out_t, spatial_w, temporal_w)
-    up = jnp.concatenate([sum1[0, :140], sum1[1, :40]], axis=0).reshape(w_up.shape).astype(F32)
-
-    def wide_of(blocks):
-        return jnp.swapaxes(blocks.reshape(4, chan, chan), 0, 1).reshape(chan, wide).astype(F32)
-
-    grad_w_out = wide_of(sum1[1, 40:120]).T
-    grad_w_in = wide_of(jnp.concatenate([sum2[0, :40], sum2[1, :40]], axis=0))
-    return (jnp.transpose(grad_skip, (2, 0, 1, 3)), up, grad_w_in, grad_w_out)
+    grad_w_out, grad_w_in = wide_grads[0].astype(F32).T, wide_grads[1].astype(F32)
+    return (jnp.transpose(grad_skip, (2, 0, 1, 3)), up.astype(F32), grad_w_in, grad_w_out)
 
 
 def solution(mesh):

time: 159 us -> 136 us (0.86)
  local copies, waits for them, and re-layouts: 22.1 us -> 8.59 us
  Pallas kernels: 133 us -> 122 us
    pallas_call x1, Pallas kernels: 133 us -> 122 us  [shards(): pl.pallas_call(main_kernel, out_shape=(jax.ShapeDtypeStruct(skip_t.shape,...]
    convert_element_type x2 -> x0, local copies, waits for them, and re-layouts: 5.72 us -> none  [wide_of(): jnp.swapaxes(blocks.reshape(4, chan, chan), 0, 1).reshape(chan, wide)]
    unnamed x7 -> x5, local copies, waits for them, and re-layouts: 8.68 us -> 3.92 us
    squeeze x2 -> x0, local copies, waits for them, and re-layouts: 2.81 us -> none  [the longest x1 1.63 us: shards(): sum1[0, :140]]
    transpose x1, other arithmetic: 0.13 us -> 1.96 us  [shards(): wide_grads[0].astype(F32)]
    transpose x2 -> x1, local copies, waits for them, and re-layouts: 3.59 us -> 4.66 us  [shards(): grad_t = jnp.transpose(grad_out, (1, 2, 0, 3))]
where the time goes in v3:
time: 136 us
  Pallas kernels  122 us (90%)
  local copies, waits for them, and re-layouts  8.59 us (6%)
  other arithmetic  4.4 us (3%)
    pallas_call x1, Pallas kernels, shards(): pl.pallas_call(main_kernel, out_shape=(jax.ShapeDtypeStruct(skip_t.shape,...  122 us
    transpose x1, local copies, waits for them, and re-layouts, shards(): grad_t = jnp.transpose(grad_out, (1, 2, 0, 3))  4.66 us
    unnamed x5, local copies, waits for them, and re-layouts  3.92 us

profile of v3, /device:TPU:1, one launch (start us, length us, event | category | flops | bytes accessed | tf_op | source)
XLA Modules:
  0.0 135.8 jit_solution(4097131675515408249)
XLA Ops:
  0.6 4.7 %copy_bitcast_fusion = (bf16[8,4,64,320]{3,2,1,0:T(8,128)(2,1)}, bf16[8,4,64,320]{3,2,1,0:T(8,128)(2,1)}) fusion(bf16[64,8,4,320]{3,2,1,0:T(4,128)(2,1)} %param.13, bf16[64,8,4,320]{3,2,1,0:T(4,128)(2,1)} %param.7), kind=kLoop, calls=%fused_computation.1 | loop fusion | bytes 5242880 | tf_op jit(solution)/shard_map/transpose | solution.py:619
  5.3 122.2 %backward.1 = (bf16[8,4,64,320]{3,2,1,0:T(8,128)(2,1)}, bf16[9,320,320]{2,1,0:T(8,128)(2,1)}, bf16[2,320,1280]{2,1,0:T(8,128)(2,1)}) custom-call(bf16[8,4,64,320]{3,2,1,0:T(8,128)(2,1)} %get-tuple-element.17.skip_hbm, bf16[8,4,64,320]{3,2,1,0:T(8,128)(2,1)} %get-tuple-element.16.grad_hbm, bf16[9,320,320]{2,1,0:T(8,128)(2,1)} %wup_hbm.1, ...), custom_call_target="tpu_custom_call" | custom-call | tf_op jit(solution)/shard_map/backward/pallas_call | solution.py:651
  127.5 0.0 copy-start
  127.5 3.9 %copy.13 = bf16[64,8,4,320]{3,2,1,0:T(4,128)(2,1)} copy(bf16[64,8,4,320]{3,0,2,1:T(8,128)(2,1)} %bitcast.14) | data formatting | bytes 2621440
  131.4 0.0 copy-done
  131.4 0.0 copy-start.1
  131.4 2.4 %convert_element_type.13 = f32[9,320,320]{2,1,0:T(8,128)} convert(bf16[9,320,320]{2,1,0:T(8,128)(2,1)S(1)} %copy-done) | non-fusion elementwise | flops 921600 | bytes 5529600 | tf_op jit(solution)/shard_map/convert_element_type | solution.py:667
  133.8 0.0 copy-done.1
  133.8 2.0 %convert_bitcast_fusion = (f32[1280,320]{0,1:T(8,128)}, f32[320,1280]{1,0:T(8,128)}) fusion(bf16[2,320,1280]{2,1,0:T(8,128)(2,1)S(1)} %copy-done.1), kind=kLoop, calls=%fused_computation | loop fusion | flops 819200 | bytes 4915200 | tf_op jit(solution)/shard_map/transpose | solution.py:666
Async XLA Ops:
  127.5 3.9 %copy-start = (bf16[9,320,320]{2,1,0:T(8,128)(2,1)S(1)}, bf16[9,320,320]{2,1,0:T(8,128)(2,1)}, u32[]{:S(2)}) copy-start(bf16[9,320,320]{2,1,0:T(8,128)(2,1)} %get-tuple-element.8) | copy-start | bytes 5529604
  131.4 2.4 %copy-start.1 = (bf16[2,320,1280]{2,1,0:T(8,128)(2,1)S(1)}, bf16[2,320,1280]{2,1,0:T(8,128)(2,1)}, u32[]{:S(2)}) copy-start(bf16[2,320,1280]{2,1,0:T(8,128)(2,1)} %get-tuple-element.9) | copy-start | bytes 4915204

commit v4 on v3

--- a/solution.py
+++ b/solution.py
@@ -310,16 +310,17 @@
     a1s, a1r, a2s, a2r, b1s, b1r, b2s, b2r, c1s, c1r, c2s, c2r, d1s, d1r, d2s, d2r,
     pooled_t, coarse_t, pooled_f, coarse_f, gunited, gexp, gexp_t, gtimed, gcoarse,
     qs, ks, vs, probs_s, qt, kt, vt, probs_t, mix, mix_t, attended, timed, gmix, gq, gk, gv, gatt,
-    unit_t,
+    unit_t, skip_raw, grad_raw,
     x1, s1, z1, p1, t1, w1, v1, a1, fin1, x2, s2, z2, p2, t2, w2, v2, a2, fin2,
     load_sem, halo_sem, swap_sem, ring_sem1, pair_sem1, ring_sem2, pair_sem2,
 ):
     r, c, g = lax.axis_index("row"), lax.axis_index("col"), lax.axis_index("grp")
+    frame_cuts = [pl.ds(8 * n, 8) for n in range(8)]
     loads = {}
     load_at = 0
     for name, pieces in (
-        ("skip", [(skip_hbm.at[i], skip.at[i]) for i in range(8)]),
-        ("grad", [(grad_hbm.at[i], gpad.at[1 + i, 1:5]) for i in range(8)]),
+        ("skip", [(skip_hbm.at[h], skip_raw.at[h]) for h in frame_cuts]),
+        ("grad", [(grad_hbm.at[h], grad_raw.at[h]) for h in frame_cuts]),
         ("win", [(win_hbm, win)]),
         ("sw", [(sw_hbm.at[m, h], sw.at[m, h]) for m in range(4) for h in cut_rows(sw, 4)]),
         ("wout", [(wout_hbm, wout)]),
@@ -331,7 +332,7 @@
              for n, (src, dst) in enumerate(pieces)]
         )
         load_at += len(pieces)
-    for name in ("skip", "grad", "win", "sw"):
+    for name in ("skip", "grad", "win", "wup", "sw", "wout", "tw"):
         loads[name].start()
 
     around = [(dr, dc) for dr in (-1, 0, 1) for dc in (-1, 0, 1) if (dr, dc) != (0, 0)]
@@ -351,7 +352,6 @@
         barrier, 1, device_id={"row": x * 2 + (r + 1) % 2, "col": (c + 4) % N}, device_id_type=MESH
     )
     pl.semaphore_signal(barrier, 1, device_id={"grp": 1 - g}, device_id_type=MESH)
-    pl.semaphore_wait(barrier, 2 * (N - 1) + 6)
     first = Sum(
         (x, y, z), g, SIZES1, x1, s1, z1, p1, t1, w1, v1, a1, fin1, ring_sem1, pair_sem1
     )
@@ -403,7 +403,19 @@
             device_id=beside(dr, dc), device_id_type=MESH,
         )
 
+    def halo_each(k, way, act):
+        tests = [
+            {-1: at > 0, 1: at < N - 1}[way * d]
+            for at, d in zip((r, c), around[k]) if d != 0
+        ]
+
+        @pl.when(tests[0] if len(tests) == 1 else jnp.logical_and(*tests))
+        def _():
+            act(halo(k))
+
     loads["skip"].wait()
+    for i in range(8):
+        skip[i] = jnp.swapaxes(skip_raw[:, i], 0, 1)
     means = []
     for p in range(2):
         total = jnp.zeros(skip.shape[2:], F32)
@@ -415,37 +427,67 @@
         rows = jnp.concatenate([means[0][8 * f:8 * f + 8], means[1][8 * f:8 * f + 8]], axis=0)
         a1s[f] = rows.astype(BF)
     pooled_t[...] = a1s[...].reshape(128, -1)
+    loads["grad"].wait()
+    for i in range(8):
+        gpad[1 + i, 1:5] = jnp.swapaxes(grad_raw[:, i], 0, 1)
+    pl.semaphore_wait(barrier, 2 * (N - 1) + 6)
     send(0, a1s, a1r, "row", r)
-    loads["grad"].wait()
-    for k in range(8):
-        halo(k).start()
-    for name in ("wout", "tw", "wup"):
-        loads[name].start()
     x1[660:] = jnp.zeros((12,) + x1.shape[1:], BF)
     x2[200:] = jnp.zeros((24,) + x2.shape[1:], BF)
     loads["win"].wait()
     coarse_t[...] = dot(pooled_t[...], win[...]).astype(BF)
     chan = gpad.shape[3]
-    gexp[...] = jnp.zeros_like(gexp)
-
-    def back_rows(first, last):
-        def step(i, carry):
-            total = jnp.zeros((256, chan), F32)
-            for dy in range(3):
-                for dx in range(3):
-                    rows = gpad[i + 2 - dy, pl.ds(2 - dx, 4)].reshape(256, chan)
-                    total = total + dot_nt(rows, wup[3 * dy + dx])
-            low = total.astype(BF)
-            gunited[i] = low.reshape(4, 64, chan)
-            gexp[i // POOL] += jnp.sum(low.astype(F32).reshape(4, 64, chan), axis=0)
-            return carry
-
-        lax.fori_loop(first, last, step, 0)
-
+    def tap_rows(tap, cols):
+        dy, dx = tap // 3, tap % 3
+        return gpad[pl.ds(2 - dy, 8), pl.ds(2 - dx, 4), :, cols].reshape(2048, -1)
+
+    def tap_step(tap, carry):
+        put(x1, 2 * tap, dot(unit_t[...], tap_rows(tap, slice(0, 256))))
+        return carry
+
+    def weight_taps(first_tap, last_tap):
+        lax.fori_loop(first_tap, last_tap, tap_step, 0)
+
+    def back_taps(rows_of, size):
+        total = jnp.zeros((size, chan), F32)
+        for dy in range(3):
+            for dx in range(3):
+                total = total + dot_nt(rows_of(dy, dx).reshape(size, chan), wup[3 * dy + dx])
+        return total.astype(BF)
+
+    def back_inner(p):
+        low = back_taps(lambda dy, dx: gpad[3 * p + 3 - dy:3 * p + 6 - dy, 3 - dx:5 - dx], 384)
+        low = low.reshape(3, 2, 64, chan)
+        gunited[3 * p + 1:3 * p + 4, 1:3] = low
+        gexp[p] = jnp.sum(low.astype(F32), axis=(0, 1))
+
+    def back_sides(p, carry):
+        def rows_of(dy, dx):
+            near = pl.ds(3 * p + 3 - dy, 3)
+            return jnp.concatenate([gpad[near, 2 - dx], gpad[near, 5 - dx]], axis=0)
+
+        low = back_taps(rows_of, 384).reshape(2, 3, 64, chan)
+        gunited[pl.ds(3 * p + 1, 3), 0] = low[0]
+        gunited[pl.ds(3 * p + 1, 3), 3] = low[1]
+        gexp[p] += jnp.sum(low.astype(F32), axis=(0, 1))
+        return carry
+
+    def back_ends(p, carry):
+        low = back_taps(lambda dy, dx: gpad[7 * p + 2 - dy, 2 - dx:6 - dx], 256)
+        low = low.reshape(4, 64, chan)
+        gunited[7 * p] = low
+        gexp[p] += jnp.sum(low.astype(F32), axis=0)
+        return carry
+
+    loads["wup"].wait()
+    back_inner(0)
     arrive(0, a1s, a1r, "row", r)
     turn(a1r, a2s, False)
     send(1, a2s, a2r, "col", c)
+    back_inner(1)
     arrive(1, a2s, a2r, "col", c)
+    for k in (3, 4):
+        halo_each(k, 1, lambda copy: copy.start())
     pooled_f[...] = a2r[...].reshape(128, chan)
 
     coarse_f[...] = dot(pooled_f[...], win[...]).astype(BF)
@@ -455,79 +497,74 @@
     attend(qs, ks, vs, probs_s, mix, None)
     b1s[...] = mix[...].reshape(b1s.shape)
     send(2, b1s, b1r, "col", c)
-    loads["wup"].wait()
-    for k in range(8):
-        halo(k).wait()
-
-    @pl.when(r == 0)
-    def _():
-        gpad[0] = jnp.zeros(gpad.shape[1:], BF)
-
-    @pl.when(r == N - 1)
-    def _():
-        gpad[9] = jnp.zeros(gpad.shape[1:], BF)
-
-    @pl.when(c == 0)
-    def _():
-        gpad[:, 0] = jnp.zeros((10,) + gpad.shape[2:], BF)
-
-    @pl.when(c == N - 1)
-    def _():
-        gpad[:, 5] = jnp.zeros((10,) + gpad.shape[2:], BF)
-
-    back_rows(0, 4)
     arrive(2, b1s, b1r, "col", c)
     turn(b1r, b2s, True)
     send(3, b2s, b2r, "row", r)
+    for k in (1, 6, 0, 2, 5, 7):
+        halo_each(k, 1, lambda copy: copy.start())
+    arrive(3, b2s, b2r, "row", r)
+    mix_t[...] = b2r[...].reshape(mix_t.shape)
+
     loads["wout"].wait()
     loads["tw"].wait()
-    back_rows(4, 8)
-    for f in range(N):
-        rows = jnp.concatenate([gexp[0, 8 * f:8 * f + 8], gexp[1, 8 * f:8 * f + 8]], axis=0)
-        gexp_t[16 * f:16 * f + 16] = rows.astype(BF)
-    gtimed[...] = dot(gexp_t[...], wout[...]).astype(BF)
-    gmix[...] = dot(gtimed[...], tw[3]).astype(BF)
-    arrive(3, b2s, b2r, "row", r)
-    mix_t[...] = b2r[...].reshape(mix_t.shape)
-
     wide_nt(coarse_t, [(mix_t, sw, 3)], attended)
     for m, ref in enumerate((qt, kt, vt)):
         ref[...] = dot(attended[...], tw[m]).astype(BF)
     row_pixel = lax.broadcasted_iota(jnp.int32, (256, 128), 0) % 16 // 8
     key_pixel = lax.broadcasted_iota(jnp.int32, (256, 128), 1) % 16 // 8
     attend(qt, kt, vt, probs_t, mix, row_pixel == key_pixel)
+    wide_nt(attended, [(mix, tw, 3)], timed)
+    expanded = dot_nt(timed[...], wout[...])
+    for p in range(2):
+        rows = jnp.concatenate(
+            [expanded[16 * f + 8 * p:16 * f + 8 * p + 8] for f in range(N)], axis=0
+        )
+
+        def unite(i, carry):
+            united = (skip[i].astype(F32) + rows[None]).astype(BF).reshape(256, chan)
+            unit_t[:, pl.ds(pl.multiple_of(i * 256, 256), 256)] = united.T
+            return carry
+
+        lax.fori_loop(p * POOL, p * POOL + POOL, unite, 0)
+    for k in range(8):
+        halo_each(k, 1, lambda copy: copy.wait_send())
+        halo_each(k, -1, lambda copy: copy.wait_recv())
+
+    @pl.when(r == 0)
+    def _():
+        gpad[0] = jnp.zeros(gpad.shape[1:], BF)
+
+    @pl.when(r == N - 1)
+    def _():
+        gpad[9] = jnp.zeros(gpad.shape[1:], BF)
+
+    @pl.when(c == 0)
+    def _():
+        gpad[:, 0] = jnp.zeros((10,) + gpad.shape[2:], BF)
+
+    @pl.when(c == N - 1)
+    def _():
+        gpad[:, 5] = jnp.zeros((10,) + gpad.shape[2:], BF)
+
+    lax.fori_loop(0, 2, back_sides, 0)
+    lax.fori_loop(0, 2, back_ends, 0)
+    for f in range(N):
+        rows = jnp.concatenate([gexp[0, 8 * f:8 * f + 8], gexp[1, 8 * f:8 * f + 8]], axis=0)
+        gexp_t[16 * f:16 * f + 16] = rows.astype(BF)
+    gtimed[...] = dot(gexp_t[...], wout[...]).astype(BF)
+    gmix[...] = dot(gtimed[...], tw[3]).astype(BF)
     attend_back(qt, kt, vt, probs_t, gmix, gq, gk, gv)
     wide_nt(gtimed, [(gq, tw, 0), (gk, tw, 1), (gv, tw, 2)], gatt)
     c1s[...] = gatt[...].reshape(c1s.shape)
     send(4, c1s, c1r, "row", r)
 
-    wide_nt(attended, [(mix, tw, 3)], timed)
     wide_tn(gexp_t, timed, x1, 23)
-    expanded = dot_nt(timed[...], wout[...])
-    for p in range(2):
-        rows = jnp.concatenate(
-            [expanded[16 * f + 8 * p:16 * f + 8 * p + 8] for f in range(N)], axis=0
-        )
-
-        def unite(i, carry):
-            united = (skip[i].astype(F32) + rows[None]).astype(BF).reshape(256, chan)
-            unit_t[:, pl.ds(pl.multiple_of(i * 256, 256), 256)] = united.T
-            return carry
-
-        lax.fori_loop(p * POOL, p * POOL + POOL, unite, 0)
+    weight_taps(0, 5)
     arrive(4, c1s, c1r, "row", r)
     turn(c1r, c2s, False)
     send(5, c2s, c2r, "col", c)
 
-    def tap_rows(tap, cols):
-        dy, dx = tap // 3, tap % 3
-        return gpad[pl.ds(2 - dy, 8), pl.ds(2 - dx, 4), :, cols].reshape(2048, -1)
-
-    def tap_step(tap, carry):
-        put(x1, 2 * tap, dot(unit_t[...], tap_rows(tap, slice(0, 256))))
-        return carry
-
-    lax.fori_loop(0, 9, tap_step, 0)
+    weight_taps(5, 9)
     for taps, at in (((0, 1, 2, 3), 18), ((4, 5, 6, 7), 20)):
         rows = jnp.concatenate([tap_rows(tap, slice(256, chan)) for tap in taps], axis=1)
         put(x1, at, dot(unit_t[...], rows))
@@ -541,24 +578,18 @@
     first.pair_add()
     first.spread_send(0)
     attend_back(qs, ks, vs, probs_s, gmix, gq, gk, gv)
-    first.spread_add(0)
-    first.spread_send(1)
     wide_nt(gatt, [(gq, sw, 0), (gk, sw, 1), (gv, sw, 2)], gcoarse)
     d1s[...] = dot_nt(gcoarse[...], win[...]).astype(BF).reshape(d1s.shape)
     send(6, d1s, d1r, "col", c)
-    first.spread_add(1)
-    first.last_send()
     wide_tn(pooled_f, gcoarse, x2, 0)
     second.pair_send()
     arrive(6, d1s, d1r, "col", c)
     turn(d1r, d2s, True)
     send(7, d2s, d2r, "row", r)
-    first.last_add()
-    first.gather_send(1)
+    first.spread_add(0)
+    first.spread_send(1)
     second.pair_add()
     second.spread_send(0)
-    first.gather_wait(1)
-    first.gather_send(0)
     arrive(7, d2s, d2r, "row", r)
     spread = d2r[...].reshape(128, chan).astype(F32) * (1.0 / (POOL * POOL))
     for p in range(2):
@@ -567,19 +598,31 @@
         )
 
         def finish(i, carry):
-            out[i] = (gunited[i].astype(F32) + rows[None]).astype(BF)
+            full = (gunited[i].astype(F32) + rows[None]).astype(BF)
+            skip_raw[:, i] = jnp.swapaxes(full, 0, 1)
             return carry
 
         lax.fori_loop(p * POOL, p * POOL + POOL, finish, 0)
+    stores = Loads([
+        pltpu.make_async_copy(skip_raw.at[h], out.at[h], load_sem.at[n])
+        for n, h in enumerate(frame_cuts)
+    ])
+    stores.start()
+    first.spread_add(1)
+    first.last_send()
     second.spread_add(0)
     second.spread_send(1)
-    first.gather_wait(0)
+    first.last_add()
+    first.gather_send(1)
     second.spread_add(1)
     second.last_send()
+    first.gather_wait(1)
+    first.gather_send(0)
     second.last_add()
     second.gather_send(1)
     second.gather_wait(1)
     second.gather_send(0)
+    first.gather_wait(0)
     second.gather_wait(0)
     first.pair_done()
 
@@ -609,14 +652,14 @@
         return carry
 
     lax.fori_loop(0, 10, wide_group2, 0)
+    stores.wait()
 
 
 def shards(skip, w_up, w_in, w_out, spatial_w, temporal_w, grad_out):
     frames, tile_h, tile_w, chan = skip.shape
     wide = w_in.shape[1]
     att = spatial_w.shape[2]
-    skip_t = jnp.transpose(skip, (1, 2, 0, 3))
-    grad_t = jnp.transpose(grad_out, (1, 2, 0, 3))
+    skip_shape = (tile_h, tile_w, frames, chan)
     w_out_t = w_out.T
 
     def vm(shape, dtype=BF):
@@ -632,17 +675,18 @@
         return [vm((n * u, 16, 128)) for n in (32, 16, 16, 4, 4, 1, 4, 4, 32)]
 
     scratch = [
-        vm(skip_t.shape), vm((tile_h + 2, tile_w + 2, frames, chan)), vm(w_up.shape),
+        vm(skip_shape), vm((tile_h + 2, tile_w + 2, frames, chan)), vm(w_up.shape),
         vm(w_in.shape), vm(w_out_t.shape), vm(spatial_w.shape), vm(temporal_w.shape),
         *swaps,
         vm((tok, chan)), vm((tok, wide)), vm((tok, chan)), vm((tok, wide)),
-        vm(skip_t.shape), vm((2, frames, chan), F32), vm((tok, chan)), vm((tok, wide)),
+        vm(skip_shape), vm((2, frames, chan), F32), vm((tok, chan)), vm((tok, wide)),
         vm((tok, wide)),
         vm((tok, att)), vm((tok, att)), vm((tok, att)), vm((att // 128, 256, 128), F32),
         vm((tok, att)), vm((tok, att)), vm((tok, att)), vm((att // 128, 256, 128), F32),
         vm((tok, att)), vm((tok, att)), vm((tok, wide)), vm((tok, wide)),
         vm((tok, att)), vm((tok, att)), vm((tok, att)), vm((tok, att)), vm((tok, wide)),
         vm((chan, frames * tile_h * tile_w)),
+        vm(skip.shape), vm(skip.shape),
         *sums(SIZES1), *sums(SIZES2),
         pltpu.SemaphoreType.DMA((59,)), pltpu.SemaphoreType.DMA((2, 8)),
         pltpu.SemaphoreType.DMA((8, 2, N)),
@@ -651,20 +695,20 @@
     grad_skip, up, wide_grads = pl.pallas_call(
         main_kernel,
         out_shape=(
-            jax.ShapeDtypeStruct(skip_t.shape, BF),
+            jax.ShapeDtypeStruct(skip.shape, BF),
             jax.ShapeDtypeStruct(w_up.shape, BF),
             jax.ShapeDtypeStruct((2,) + w_in.shape, BF),
         ),
         in_specs=[pl.BlockSpec(memory_space=pl.ANY)] * 7,
-        out_specs=[pl.BlockSpec(memory_space=pltpu.VMEM)] * 3,
+        out_specs=[pl.BlockSpec(memory_space=pl.ANY)] + [pl.BlockSpec(memory_space=pltpu.VMEM)] * 2,
         scratch_shapes=scratch,
         compiler_params=pltpu.CompilerParams(
             collective_id=0, has_side_effects=True, vmem_limit_bytes=60 * 1024 * 1024
         ),
         name="backward",
-    )(skip_t, grad_t, w_up, w_in, w_out_t, spatial_w, temporal_w)
+    )(skip, grad_out, w_up, w_in, w_out_t, spatial_w, temporal_w)
     grad_w_out, grad_w_in = wide_grads[0].astype(F32).T, wide_grads[1].astype(F32)
-    return (jnp.transpose(grad_skip, (2, 0, 1, 3)), up.astype(F32), grad_w_in, grad_w_out)
+    return (grad_skip, up.astype(F32), grad_w_in, grad_w_out)
 
 
 def solution(mesh):

time: 136 us -> 123 us (0.904)
  local copies, waits for them, and re-layouts: 8.59 us -> 1.15 us
  Pallas kernels: 122 us -> 115 us
  other arithmetic: 4.4 us -> 6.14 us
    pallas_call x1, Pallas kernels: 122 us -> 115 us  [shards(): pl.pallas_call(main_kernel, out_shape=(jax.ShapeDtypeStruct(skip.shape, B...]
    transpose x1 -> x0, local copies, waits for them, and re-layouts: 4.66 us -> none  [shards(): grad_t = jnp.transpose(grad_out, (1, 2, 0, 3))]
    unnamed x5, local copies, waits for them, and re-layouts: 3.92 us -> 1.15 us
    convert_element_type x1, other arithmetic: 2.44 us -> 4.19 us  [shards(): return (grad_skip, up.astype(F32), grad_w_in, grad_w_out)]
where the time goes in v4:
time: 123 us
  Pallas kernels  115 us (93%)
  other arithmetic  6.14 us (5%)
    pallas_call x1, Pallas kernels, shards(): pl.pallas_call(main_kernel, out_shape=(jax.ShapeDtypeStruct(skip.shape, B...  115 us
    convert_element_type x1, other arithmetic, shards(): return (grad_skip, up.astype(F32), grad_w_in, grad_w_out)  4.19 us

profile of v4, /device:TPU:1, one launch (start us, length us, event | category | flops | bytes accessed | tf_op | source)
XLA Modules:
  0.0 123.4 jit_solution(13880323471024699060)
XLA Ops:
  0.6 115.4 %backward.1 = (bf16[64,8,4,320]{3,2,1,0:T(4,128)(2,1)}, bf16[9,320,320]{2,1,0:T(8,128)(2,1)}, bf16[2,320,1280]{2,1,0:T(8,128)(2,1)}) custom-call(bf16[64,8,4,320]{3,2,1,0:T(4,128)(2,1)} %skip_hbm.1, bf16[64,8,4,320]{3,2,1,0:T(4,128)(2,1)} %grad_hbm.1, bf16[9,320,320]{2,1,0:T(8,128)(2,1)} %wup_hbm.1, bf16[320,1280]{1,0:T(8,128)(2,1)} %win_hbm.1, ...), custom_call_target="tpu_custom_call" | custom-call | tf_op jit(solution)/shard_map/backward/pallas_call | solution.py:695
  116.1 0.0 copy-start
  116.1 4.2 %convert_element_type.13 = f32[9,320,320]{2,1,0:T(8,128)} convert(bf16[9,320,320]{2,1,0:T(8,128)(2,1)} %get-tuple-element.8) | non-fusion elementwise | flops 921600 | bytes 5529600 | tf_op jit(solution)/shard_map/convert_element_type | solution.py:711
  120.3 0.0 copy-done
  120.3 0.0 copy-start.1
  120.3 2.0 %convert_bitcast_fusion = (f32[1280,320]{0,1:T(8,128)}, f32[320,1280]{1,0:T(8,128)}) fusion(bf16[2,320,1280]{2,1,0:T(8,128)(2,1)S(1)} %copy-done), kind=kLoop, calls=%fused_computation | loop fusion | flops 819200 | bytes 4915200 | tf_op jit(solution)/shard_map/transpose | solution.py:710
  122.2 0.0 copy-done.1
  122.2 1.1 copy.12
Async XLA Ops:
  116.1 4.2 %copy-start = (bf16[2,320,1280]{2,1,0:T(8,128)(2,1)S(1)}, bf16[2,320,1280]{2,1,0:T(8,128)(2,1)}, u32[]{:S(2)}) copy-start(bf16[2,320,1280]{2,1,0:T(8,128)(2,1)} %get-tuple-element.9) | copy-start | bytes 4915204
  120.3 2.0 %copy-start.1 = (bf16[64,8,4,320]{3,2,1,0:T(4,128)(2,1)S(1)}, bf16[64,8,4,320]{3,2,1,0:T(4,128)(2,1)}, u32[]{:S(2)}) copy-start(bf16[64,8,4,320]{3,2,1,0:T(4,128)(2,1)} %get-tuple-element.16) | copy-start | bytes 3932164

commit v5 on v4

--- a/solution.py
+++ b/solution.py
@@ -155,14 +155,13 @@
         )
 
     def others(self, stage, step):
-        for k in range(3):
-            me = self.me(k, stage)
-
-            def one(d, carry):
-                step(k, me, (me + d) % 4)
-                return carry
-
-            lax.fori_loop(1, 4, one, 0)
+        def one(d, carry):
+            for k in range(3):
+                me = self.me(k, stage)
+                step(k, me, (me + d % 3 + 1) % 4)
+            return carry
+
+        lax.fori_loop(1, 4, one, 0)
 
     def quarters(self, step):
         for k in range(3):
@@ -579,17 +578,27 @@
     first.spread_send(0)
     attend_back(qs, ks, vs, probs_s, gmix, gq, gk, gv)
     wide_nt(gatt, [(gq, sw, 0), (gk, sw, 1), (gv, sw, 2)], gcoarse)
-    d1s[...] = dot_nt(gcoarse[...], win[...]).astype(BF).reshape(d1s.shape)
-    send(6, d1s, d1r, "col", c)
     wide_tn(pooled_f, gcoarse, x2, 0)
     second.pair_send()
+    d1s[...] = dot_nt(gcoarse[...], win[...]).astype(BF).reshape(d1s.shape)
+    first.spread_add(0)
+    first.spread_send(1)
+    send(6, d1s, d1r, "col", c)
+    second.pair_add()
+    second.spread_send(0)
+    first.spread_add(1)
+    first.last_send()
     arrive(6, d1s, d1r, "col", c)
     turn(d1r, d2s, True)
     send(7, d2s, d2r, "row", r)
-    first.spread_add(0)
-    first.spread_send(1)
-    second.pair_add()
-    second.spread_send(0)
+    first.last_add()
+    first.gather_send(1)
+    second.spread_add(0)
+    second.spread_send(1)
+    first.gather_wait(1)
+    first.gather_send(0)
+    second.spread_add(1)
+    second.last_send()
     arrive(7, d2s, d2r, "row", r)
     spread = d2r[...].reshape(128, chan).astype(F32) * (1.0 / (POOL * POOL))
     for p in range(2):
@@ -608,16 +617,6 @@
         for n, h in enumerate(frame_cuts)
     ])
     stores.start()
-    first.spread_add(1)
-    first.last_send()
-    second.spread_add(0)
-    second.spread_send(1)
-    first.last_add()
-    first.gather_send(1)
-    second.spread_add(1)
-    second.last_send()
-    first.gather_wait(1)
-    first.gather_send(0)
     second.last_add()
     second.gather_send(1)
     second.gather_wait(1)

time: 123 us -> 121 us (0.984)
  Pallas kernels: 115 us -> 113 us
    pallas_call x1, Pallas kernels: 115 us -> 113 us  [shards(): pl.pallas_call(main_kernel, out_shape=(jax.ShapeDtypeStruct(skip.shape, B...]
where the time goes in v5:
time: 121 us
  Pallas kernels  113 us (93%)
  other arithmetic  6.14 us (5%)
    pallas_call x1, Pallas kernels, shards(): pl.pallas_call(main_kernel, out_shape=(jax.ShapeDtypeStruct(skip.shape, B...  113 us
    convert_element_type x1, other arithmetic, shards(): return (grad_skip, up.astype(F32), grad_w_in, grad_w_out)  4.19 us

profile of v5, /device:TPU:1, one launch (start us, length us, event | category | flops | bytes accessed | tf_op | source)
XLA Modules:
  0.0 120.8 jit_solution(12228648610673076109)
XLA Ops:
  0.6 112.8 %backward.1 = (bf16[64,8,4,320]{3,2,1,0:T(4,128)(2,1)}, bf16[9,320,320]{2,1,0:T(8,128)(2,1)}, bf16[2,320,1280]{2,1,0:T(8,128)(2,1)}) custom-call(bf16[64,8,4,320]{3,2,1,0:T(4,128)(2,1)} %skip_hbm.1, bf16[64,8,4,320]{3,2,1,0:T(4,128)(2,1)} %grad_hbm.1, bf16[9,320,320]{2,1,0:T(8,128)(2,1)} %wup_hbm.1, bf16[320,1280]{1,0:T(8,128)(2,1)} %win_hbm.1, ...), custom_call_target="tpu_custom_call" | custom-call | tf_op jit(solution)/shard_map/backward/pallas_call | solution.py:694
  113.5 0.0 copy-start
  113.5 4.2 %convert_element_type.13 = f32[9,320,320]{2,1,0:T(8,128)} convert(bf16[9,320,320]{2,1,0:T(8,128)(2,1)} %get-tuple-element.8) | non-fusion elementwise | flops 921600 | bytes 5529600 | tf_op jit(solution)/shard_map/convert_element_type | solution.py:710
  117.7 0.0 copy-done
  117.7 0.0 copy-start.1
  117.7 2.0 %convert_bitcast_fusion = (f32[1280,320]{0,1:T(8,128)}, f32[320,1280]{1,0:T(8,128)}) fusion(bf16[2,320,1280]{2,1,0:T(8,128)(2,1)S(1)} %copy-done), kind=kLoop, calls=%fused_computation | loop fusion | flops 819200 | bytes 4915200 | tf_op jit(solution)/shard_map/transpose | solution.py:709
  119.6 0.0 copy-done.1
  119.6 1.1 copy.12
Async XLA Ops:
  113.5 4.2 %copy-start = (bf16[2,320,1280]{2,1,0:T(8,128)(2,1)S(1)}, bf16[2,320,1280]{2,1,0:T(8,128)(2,1)}, u32[]{:S(2)}) copy-start(bf16[2,320,1280]{2,1,0:T(8,128)(2,1)} %get-tuple-element.9) | copy-start | bytes 4915204
  117.7 2.0 %copy-start.1 = (bf16[64,8,4,320]{3,2,1,0:T(4,128)(2,1)S(1)}, bf16[64,8,4,320]{3,2,1,0:T(4,128)(2,1)}, u32[]{:S(2)}) copy-start(bf16[64,8,4,320]{3,2,1,0:T(4,128)(2,1)} %get-tuple-element.16) | copy-start | bytes 3932164
